TPU v7x, 128 devices: a whole 4x4x4 slice. The times are simulated.
128 devices in a mesh: ctx: 32 (over y_lo, z, x), fsdp: 4 (over y_hi, core).
Axes of the slice: x: 4, y: 4 (y_hi: 2, y_lo: 2; y = y_hi * 2 + y_lo), z: 4, core: 2. Of those that a mesh axis runs over, the one named last changes fastest.
Arguments:
- tokens: bfloat16 [4, 2, 4096, 640], P('fsdp', None, 'ctx'), may hold values from -6 to 6
- cotangent: bfloat16 [4, 2, 4096, 640], P('fsdp', None, 'ctx'), may hold values from -6 to 6
- lengths: int32 [4, 2], P('fsdp'), may hold values from 1024 to 4096, as said below
- block_order: int32 [64], replicated, may hold values from 0 to 63, each once
- query_weight: bfloat16 [640, 1024], P(None, 'fsdp'), may hold values from -0.25 to 0.25
- key_weight: bfloat16 [640, 256], P(None, 'fsdp'), may hold values from -0.25 to 0.25
- value_weight: bfloat16 [640, 256], P(None, 'fsdp'), may hold values from -0.25 to 0.25
- out_weight: bfloat16 [1024, 640], P('fsdp'), may hold values from -0.1875 to 0.1875
- gate_weight: bfloat16 [640, 2048], P(None, 'fsdp'), may hold values from -0.25 to 0.25
- up_weight: bfloat16 [640, 2048], P(None, 'fsdp'), may hold values from -0.25 to 0.25
- down_weight: bfloat16 [2048, 640], P('fsdp'), may hold values from -0.125 to 0.125
- gain_attn_in: bfloat16 [640], P('fsdp'), may hold values from -0.5 to 0.5
- gain_attn_out: bfloat16 [640], P('fsdp'), may hold values from -0.5 to 0.5
- gain_ffn_in: bfloat16 [640], P('fsdp'), may hold values from -0.5 to 0.5
- gain_ffn_out: bfloat16 [640], P('fsdp'), may hold values from -0.5 to 0.5
Outputs:
- result: bfloat16 [4, 2, 4096, 640], P('fsdp', None, 'ctx')
- token_grad: float32 [4, 2, 4096, 640], P('fsdp', None, 'ctx')
- query_grad: float32 [640, 1024], P(None, 'fsdp')
- key_grad: float32 [640, 256], P(None, 'fsdp')
- value_grad: float32 [640, 256], P(None, 'fsdp')
- out_grad: float32 [1024, 640], P('fsdp')
- gate_grad: float32 [640, 2048], P(None, 'fsdp')
- up_grad: float32 [640, 2048], P(None, 'fsdp')
- down_grad: float32 [2048, 640], P('fsdp')
- attn_in_grad: float32 [640], P('fsdp')
- attn_out_grad: float32 [640], P('fsdp')
- ffn_in_grad: float32 [640], P('fsdp')
- ffn_out_grad: float32 [640], P('fsdp')
Inputs may be any that keep to these rules, and one draw needn't show every extreme that they name: `lengths`: in each group the sequence of one micro-batch, drawn from the seed, has exactly 4096 valid tokens; in one group, drawn from the seed, another sequence has exactly 1024.
All inputs are finite; a program needn't handle non-finite values.
Results may differ from a plain program's by a relative error of at most 0.03.
Values may be sent and summed in bfloat16 or wider, within the bound.
No kernel may reach another device: no remote copies, remote signals or barrier semaphores. Data moves between devices by JAX's collectives and lax.ppermute only.
A program may use at most 192 MiB of HBM per device.

v0:
```python
import jax
import jax.numpy as jnp
from jax import lax
from jax.sharding import PartitionSpec as P

MB = 2


cap_limit = 50.0
norm_eps = 1e-06
rope_base = 1000000.0
masked_value = -1000000000.0


def normalize(values, gain):
    scale = lax.rsqrt(jnp.mean(values * values, axis=-1, keepdims=True) + norm_eps)
    return values * scale * (1.0 + gain)


def gelu_product(gate_value, upward):
    return jax.nn.gelu(gate_value, approximate=True) * upward


def rotation_tables(positions, head_size):
    half_size = head_size // 2
    freqs = rope_base ** (-(jnp.arange(half_size).astype(jnp.float32) * 2.0 / head_size))
    angles = positions.astype(jnp.float32)[:, None] * freqs[None, :]
    return (jnp.cos(angles), jnp.sin(angles))


def rotate(values, cosine, sine_table):
    half_size = values.shape[-1] // 2
    first_half = values[..., :half_size]
    second_half = values[..., half_size:]
    return jnp.concatenate(
        [
            first_half * cosine - second_half * sine_table,
            second_half * cosine + first_half * sine_table,
        ],
        axis=-1,
    )


def unrotate(grads_in, cosine, sine_table):
    half_size = grads_in.shape[-1] // 2
    first_half = grads_in[..., :half_size]
    second_half = grads_in[..., half_size:]
    return jnp.concatenate(
        [
            first_half * cosine + second_half * sine_table,
            second_half * cosine - first_half * sine_table,
        ],
        axis=-1,
    )


def micro_step(inputs, incoming, length, full_weights, shard_list, positions_own, positions_all):
    (
        query_weight,
        key_weight,
        value_weight,
        out_weight,
        gate_weight,
        up_weight,
        down_weight,
        gain_a,
        gain_b,
        gain_c,
        gain_d,
    ) = full_weights
    row_count = inputs.shape[0]
    heads_total = query_weight.shape[1]
    head_size = key_weight.shape[1]
    head_count = heads_total // head_size
    scale_query = head_size ** (-0.5)
    gain_a = gain_a.astype(jnp.float32)
    gain_b = gain_b.astype(jnp.float32)
    gain_c = gain_c.astype(jnp.float32)
    gain_d = gain_d.astype(jnp.float32)
    start_rows = inputs.astype(jnp.float32)
    cosine, sine_table = rotation_tables(positions_own, head_size)
    normed = normalize(start_rows, gain_a).astype(jnp.bfloat16)
    query_pre = jnp.dot(normed, query_weight, preferred_element_type=jnp.float32)
    key_pre = jnp.dot(normed, key_weight, preferred_element_type=jnp.float32)
    value_pre = jnp.dot(normed, value_weight, preferred_element_type=jnp.float32)
    queries = (
        rotate(
            query_pre.reshape(row_count, head_count, head_size),
            cosine[:, None, :],
            sine_table[:, None, :],
        )
        * scale_query
    ).astype(jnp.bfloat16)
    key_rows = rotate(key_pre, cosine, sine_table).astype(jnp.bfloat16)
    value_rows = value_pre.astype(jnp.bfloat16)
    all_keys, all_values = (
        lax.all_gather(key_rows, "ctx", axis=0, tiled=True),
        lax.all_gather(value_rows, "ctx", axis=0, tiled=True),
    )
    scores = jnp.einsum("qhd,kd->hqk", queries, all_keys, preferred_element_type=jnp.float32)
    tanh_ratio = jnp.tanh(scores / cap_limit)
    allowed = (positions_all[None, :] <= positions_own[:, None]) & (positions_all < length)[None, :]
    capped = jnp.where(allowed[None], cap_limit * tanh_ratio, masked_value)
    row_top = jnp.max(capped, axis=-1, keepdims=True)
    row_total = jnp.log(jnp.sum(jnp.exp(capped - row_top), axis=-1, keepdims=True)) + row_top
    weights_soft = jnp.exp(capped - row_total)
    weights_low = weights_soft.astype(jnp.bfloat16)
    mixed = jnp.einsum("hqk,kd->qhd", weights_low, all_values, preferred_element_type=jnp.float32)
    attended = mixed.reshape(row_count, heads_total).astype(jnp.bfloat16)
    branch = jnp.dot(attended, out_weight, preferred_element_type=jnp.float32)
    middle = start_rows + normalize(branch, gain_b)
    second = normalize(middle, gain_c).astype(jnp.bfloat16)
    gate_value = jnp.dot(second, gate_weight, preferred_element_type=jnp.float32)
    upward = jnp.dot(second, up_weight, preferred_element_type=jnp.float32)
    hidden = gelu_product(gate_value, upward).astype(jnp.bfloat16)
    output = jnp.dot(hidden, down_weight, preferred_element_type=jnp.float32)
    valid_rows = (positions_own < length)[:, None]
    result_rows = jnp.where(valid_rows, middle + normalize(output, gain_d), 0.0).astype(
        jnp.bfloat16
    )
    (
        shard_q,
        shard_k,
        shard_v,
        shard_o,
        shard_g,
        shard_u,
        shard_d,
        shard_ga,
        shard_gb,
        shard_gc,
        shard_gd,
    ) = shard_list
    back_weights = (
        lax.all_gather(shard_q, "fsdp", axis=1, tiled=True),
        lax.all_gather(shard_k, "fsdp", axis=1, tiled=True),
        lax.all_gather(shard_v, "fsdp", axis=1, tiled=True),
        lax.all_gather(shard_o, "fsdp", axis=0, tiled=True),
        lax.all_gather(shard_g, "fsdp", axis=1, tiled=True),
        lax.all_gather(shard_u, "fsdp", axis=1, tiled=True),
        lax.all_gather(shard_d, "fsdp", axis=0, tiled=True),
        lax.all_gather(shard_ga, "fsdp", axis=0, tiled=True),
        lax.all_gather(shard_gb, "fsdp", axis=0, tiled=True),
        lax.all_gather(shard_gc, "fsdp", axis=0, tiled=True),
        lax.all_gather(shard_gd, "fsdp", axis=0, tiled=True),
    )
    query_weight, key_weight, value_weight, out_weight, gate_weight, up_weight, down_weight = (
        back_weights[:7]
    )
    grad_seed = jnp.where(valid_rows, incoming.astype(jnp.float32), 0.0)
    _, pull_out = jax.vjp(normalize, output, gain_d)
    d_output, d_gain_d = pull_out(grad_seed)
    d_output_low = d_output.astype(jnp.bfloat16)
    grad_down = jnp.einsum("rf,rd->fd", hidden, d_output_low, preferred_element_type=jnp.float32)
    d_hidden = jnp.einsum(
        "rd,fd->rf", d_output_low, down_weight, preferred_element_type=jnp.float32
    )
    _, pull_gelu = jax.vjp(gelu_product, gate_value, upward)
    d_gate, d_upward = pull_gelu(d_hidden)
    d_gate_low = d_gate.astype(jnp.bfloat16)
    d_upward_low = d_upward.astype(jnp.bfloat16)
    grad_gate = jnp.einsum("rd,rf->df", second, d_gate_low, preferred_element_type=jnp.float32)
    grad_up = jnp.einsum("rd,rf->df", second, d_upward_low, preferred_element_type=jnp.float32)
    d_second = jnp.einsum(
        "rf,df->rd", d_gate_low, gate_weight, preferred_element_type=jnp.float32
    ) + jnp.einsum("rf,df->rd", d_upward_low, up_weight, preferred_element_type=jnp.float32)
    _, pull_mid = jax.vjp(normalize, middle, gain_c)
    d_mid_norm, d_gain_c = pull_mid(d_second)
    d_middle = grad_seed + d_mid_norm
    _, pull_branch = jax.vjp(normalize, branch, gain_b)
    d_branch, d_gain_b = pull_branch(d_middle)
    d_branch_low = d_branch.astype(jnp.bfloat16)
    grad_out = jnp.einsum("ra,rd->ad", attended, d_branch_low, preferred_element_type=jnp.float32)
    d_attended = (
        jnp.einsum("rd,ad->ra", d_branch_low, out_weight, preferred_element_type=jnp.float32)
        .astype(jnp.bfloat16)
        .reshape(row_count, head_count, head_size)
    )
    d_weights = jnp.einsum(
        "qhd,kd->hqk", d_attended, all_values, preferred_element_type=jnp.float32
    )
    center = jnp.sum(weights_soft * d_weights, axis=-1, keepdims=True)
    d_capped = weights_soft * (d_weights - center)
    d_scores = (d_capped * (1.0 - tanh_ratio * tanh_ratio)).astype(jnp.bfloat16)
    d_queries = jnp.einsum("hqk,kd->qhd", d_scores, all_keys, preferred_element_type=jnp.float32)
    key_terms = jnp.einsum("hqk,qhd->kd", d_scores, queries, preferred_element_type=jnp.float32)
    value_terms = jnp.einsum(
        "hqk,qhd->kd", weights_low, d_attended, preferred_element_type=jnp.float32
    )
    d_keys, d_values = (
        lax.psum_scatter(
            key_terms.astype(jnp.bfloat16), "ctx", scatter_dimension=0, tiled=True
        ).astype(jnp.float32),
        lax.psum_scatter(
            value_terms.astype(jnp.bfloat16), "ctx", scatter_dimension=0, tiled=True
        ).astype(jnp.float32),
    )
    d_query_pre = (
        unrotate(d_queries * scale_query, cosine[:, None, :], sine_table[:, None, :])
        .reshape(row_count, heads_total)
        .astype(jnp.bfloat16)
    )
    d_key_pre = unrotate(d_keys, cosine, sine_table).astype(jnp.bfloat16)
    d_value_pre = d_values.astype(jnp.bfloat16)
    grad_query = jnp.einsum("rd,ra->da", normed, d_query_pre, preferred_element_type=jnp.float32)
    grad_key = jnp.einsum("rd,ra->da", normed, d_key_pre, preferred_element_type=jnp.float32)
    grad_value = jnp.einsum("rd,ra->da", normed, d_value_pre, preferred_element_type=jnp.float32)
    d_normed = jnp.einsum(
        "ra,da->rd", d_query_pre, query_weight, preferred_element_type=jnp.float32
    )
    d_normed = d_normed + jnp.einsum(
        "ra,da->rd", d_key_pre, key_weight, preferred_element_type=jnp.float32
    )
    d_normed = d_normed + jnp.einsum(
        "ra,da->rd", d_value_pre, value_weight, preferred_element_type=jnp.float32
    )
    _, pull_start = jax.vjp(normalize, start_rows, gain_a)
    d_start, d_gain_a = pull_start(d_normed)
    token_rows = d_middle + d_start
    grads = (
        grad_query,
        grad_key,
        grad_value,
        grad_out,
        grad_gate,
        grad_up,
        grad_down,
        d_gain_a,
        d_gain_b,
        d_gain_c,
        d_gain_d,
    )
    return (result_rows, token_rows, grads)


def on_device(
    tokens,
    cotangent,
    lengths,
    block_order,
    query_weight,
    key_weight,
    value_weight,
    out_weight,
    gate_weight,
    up_weight,
    down_weight,
    gain_attn_in,
    gain_attn_out,
    gain_ffn_in,
    gain_ffn_out,
):
    shard_list = (
        query_weight,
        key_weight,
        value_weight,
        out_weight,
        gate_weight,
        up_weight,
        down_weight,
        gain_attn_in,
        gain_attn_out,
        gain_ffn_in,
        gain_ffn_out,
    )
    local_slots = tokens.shape[2]
    block_rows = local_slots // 2
    context_index = lax.axis_index("ctx")
    inner = jnp.arange(block_rows, dtype=jnp.int32)
    positions_all = (block_order[:, None] * block_rows + inner[None, :]).reshape(-1)
    positions_own = lax.dynamic_slice_in_dim(
        positions_all, context_index * local_slots, local_slots
    )
    result_list = []
    token_list = []
    shard_totals = None
    for micro_index in range(MB):
        full_weights = (
            lax.all_gather(query_weight, "fsdp", axis=1, tiled=True),
            lax.all_gather(key_weight, "fsdp", axis=1, tiled=True),
            lax.all_gather(value_weight, "fsdp", axis=1, tiled=True),
            lax.all_gather(out_weight, "fsdp", axis=0, tiled=True),
            lax.all_gather(gate_weight, "fsdp", axis=1, tiled=True),
            lax.all_gather(up_weight, "fsdp", axis=1, tiled=True),
            lax.all_gather(down_weight, "fsdp", axis=0, tiled=True),
            lax.all_gather(gain_attn_in, "fsdp", axis=0, tiled=True),
            lax.all_gather(gain_attn_out, "fsdp", axis=0, tiled=True),
            lax.all_gather(gain_ffn_in, "fsdp", axis=0, tiled=True),
            lax.all_gather(gain_ffn_out, "fsdp", axis=0, tiled=True),
        )
        result_rows, token_rows, grads = micro_step(
            tokens[0, micro_index],
            cotangent[0, micro_index],
            lengths[0, micro_index],
            full_weights,
            shard_list,
            positions_own,
            positions_all,
        )
        result_list.append(result_rows)
        token_list.append(token_rows)
        (
            term_q,
            term_k,
            term_v,
            term_o,
            term_g,
            term_u,
            term_d,
            term_ga,
            term_gb,
            term_gc,
            term_gd,
        ) = grads
        pieces = (
            lax.psum_scatter(
                term_q.astype(jnp.bfloat16), "fsdp", scatter_dimension=1, tiled=True
            ).astype(jnp.float32),
            lax.psum_scatter(
                term_k.astype(jnp.bfloat16), "fsdp", scatter_dimension=1, tiled=True
            ).astype(jnp.float32),
            lax.psum_scatter(
                term_v.astype(jnp.bfloat16), "fsdp", scatter_dimension=1, tiled=True
            ).astype(jnp.float32),
            lax.psum_scatter(
                term_o.astype(jnp.bfloat16), "fsdp", scatter_dimension=0, tiled=True
            ).astype(jnp.float32),
            lax.psum_scatter(
                term_g.astype(jnp.bfloat16), "fsdp", scatter_dimension=1, tiled=True
            ).astype(jnp.float32),
            lax.psum_scatter(
                term_u.astype(jnp.bfloat16), "fsdp", scatter_dimension=1, tiled=True
            ).astype(jnp.float32),
            lax.psum_scatter(
                term_d.astype(jnp.bfloat16), "fsdp", scatter_dimension=0, tiled=True
            ).astype(jnp.float32),
            lax.psum_scatter(
                term_ga.astype(jnp.bfloat16), "fsdp", scatter_dimension=0, tiled=True
            ).astype(jnp.float32),
            lax.psum_scatter(
                term_gb.astype(jnp.bfloat16), "fsdp", scatter_dimension=0, tiled=True
            ).astype(jnp.float32),
            lax.psum_scatter(
                term_gc.astype(jnp.bfloat16), "fsdp", scatter_dimension=0, tiled=True
            ).astype(jnp.float32),
            lax.psum_scatter(
                term_gd.astype(jnp.bfloat16), "fsdp", scatter_dimension=0, tiled=True
            ).astype(jnp.float32),
        )
        (
            piece_q,
            piece_k,
            piece_v,
            piece_o,
            piece_g,
            piece_u,
            piece_d,
            piece_ga,
            piece_gb,
            piece_gc,
            piece_gd,
        ) = pieces
        summed = (
            lax.psum(piece_q.astype(jnp.bfloat16), "ctx").astype(jnp.float32),
            lax.psum(piece_k.astype(jnp.bfloat16), "ctx").astype(jnp.float32),
            lax.psum(piece_v.astype(jnp.bfloat16), "ctx").astype(jnp.float32),
            lax.psum(piece_o.astype(jnp.bfloat16), "ctx").astype(jnp.float32),
            lax.psum(piece_g.astype(jnp.bfloat16), "ctx").astype(jnp.float32),
            lax.psum(piece_u.astype(jnp.bfloat16), "ctx").astype(jnp.float32),
            lax.psum(piece_d.astype(jnp.bfloat16), "ctx").astype(jnp.float32),
            lax.psum(piece_ga.astype(jnp.bfloat16), "ctx").astype(jnp.float32),
            lax.psum(piece_gb.astype(jnp.bfloat16), "ctx").astype(jnp.float32),
            lax.psum(piece_gc.astype(jnp.bfloat16), "ctx").astype(jnp.float32),
            lax.psum(piece_gd.astype(jnp.bfloat16), "ctx").astype(jnp.float32),
        )
        if shard_totals is None:
            shard_totals = tuple(summed)
        else:
            shard_totals = tuple((left + right for left, right in zip(shard_totals, summed)))
    result_block = jnp.stack(result_list)[None]
    token_block = jnp.stack(token_list)[None]
    return (
        result_block,
        token_block,
        shard_totals[0],
        shard_totals[1],
        shard_totals[2],
        shard_totals[3],
        shard_totals[4],
        shard_totals[5],
        shard_totals[6],
        shard_totals[7],
        shard_totals[8],
        shard_totals[9],
        shard_totals[10],
    )


def solution(mesh):
    placed = (
        P("fsdp", None, "ctx", None),
        P("fsdp", None, "ctx", None),
        P("fsdp", None),
        P(),
        P(None, "fsdp"),
        P(None, "fsdp"),
        P(None, "fsdp"),
        P("fsdp", None),
        P(None, "fsdp"),
        P(None, "fsdp"),
        P("fsdp", None),
        P("fsdp"),
        P("fsdp"),
        P("fsdp"),
        P("fsdp"),
    )
    return jax.shard_map(
        on_device,
        mesh=mesh,
        in_specs=placed,
        out_specs=(
            P("fsdp", None, "ctx", None),
            P("fsdp", None, "ctx", None),
            P(None, "fsdp"),
            P(None, "fsdp"),
            P(None, "fsdp"),
            P("fsdp", None),
            P(None, "fsdp"),
            P(None, "fsdp"),
            P("fsdp", None),
            P("fsdp"),
            P("fsdp"),
            P("fsdp"),
            P("fsdp"),
        ),
        check_vma=False,
    )
```

profile of v0, /device:TPU:1, one launch (start us, length us, event | category | flops | bytes accessed | tf_op | source)
XLA Modules:
  0.0 2305.9 jit_solution(7364472317462870416)
XLA Ops:
  66.2 107.0 %all-gather.12.cloned.1.call-done = bf16[4096,256]{1,0:T(8,128)(2,1)} async-done(((bf16[128,256]{1,0:T(8,128)(2,1)}), bf16[4096,256]{1,0:T(8,128)(2,1)}) %all-gather.12.cloned.1.call-update) | async-done | bytes 2097168 | tf_op jit(solution)/shard_map/all_gather | solution.py:97
  182.7 146.1 %all-gather.10.cloned.1.call-done = bf16[4096,256]{1,0:T(8,128)(2,1)} async-done(((bf16[128,256]{1,0:T(8,128)(2,1)}), bf16[4096,256]{1,0:T(8,128)(2,1)}) %all-gather.10.cloned.1.call-update) | async-done | bytes 2097168 | tf_op jit(solution)/shard_map/all_gather | solution.py:98
  335.8 37.9 %all-gather.16.cloned.1.call-done = bf16[1024,640]{1,0:T(8,128)(2,1)} async-done(((bf16[256,640]{1,0:T(8,128)(2,1)}), bf16[1024,640]{1,0:T(8,128)(2,1)}) %all-gather.16.cloned.1.call-update) | async-done | bytes 1310736 | tf_op jit(solution)/shard_map/all_gather | solution.py:282
  375.6 131.8 %all-gather.26.cloned.1.call-done = bf16[4096,256]{1,0:T(8,128)(2,1)} async-done(((bf16[128,256]{1,0:T(8,128)(2,1)}), bf16[4096,256]{1,0:T(8,128)(2,1)}) %all-gather.26.cloned.1.call-update) | async-done | bytes 2097168 | tf_op jit(solution)/shard_map/all_gather | solution.py:97
  514.2 148.6 %all-gather.24.cloned.1.call-done = bf16[4096,256]{1,0:T(8,128)(2,1)} async-done(((bf16[128,256]{1,0:T(8,128)(2,1)}), bf16[4096,256]{1,0:T(8,128)(2,1)}) %all-gather.24.cloned.1.call-update) | async-done | bytes 2097168 | tf_op jit(solution)/shard_map/all_gather | solution.py:98
  672.3 43.0 %all-gather.18.cloned.1.call-done = bf16[640,2048]{1,0:T(8,128)(2,1)} async-done(((bf16[640,512]{1,0:T(8,128)(2,1)}), bf16[640,2048]{1,0:T(8,128)(2,1)}) %all-gather.18.cloned.1.call-update) | async-done | bytes 2621456 | tf_op jit(solution)/shard_map/all_gather | solution.py:283
  718.7 27.3 %all-gather.20.cloned.1.call-done = bf16[640,2048]{1,0:T(8,128)(2,1)} async-done(((bf16[640,512]{1,0:T(8,128)(2,1)}), bf16[640,2048]{1,0:T(8,128)(2,1)}) %all-gather.20.cloned.1.call-update) | async-done | bytes 2621456 | tf_op jit(solution)/shard_map/all_gather | solution.py:284
  750.0 26.8 %all-gather.22.cloned.1.call-done = bf16[2048,640]{1,0:T(8,128)(2,1)} async-done(((bf16[512,640]{1,0:T(8,128)(2,1)}), bf16[2048,640]{1,0:T(8,128)(2,1)}) %all-gather.22.cloned.1.call-update) | async-done | bytes 2621456 | tf_op jit(solution)/shard_map/all_gather | solution.py:285
  814.8 18.9 fusion.12
  840.2 19.1 fusion.10
  863.1 18.3 fusion.79
  881.4 19.7 fusion.85
  911.2 27.0 %reduce-scatter.21.cloned.1.call-done = bf16[128,256]{1,0:T(8,128)(2,1)} async-done(((bf16[4096,256]{1,0:T(8,128)(2,1)}), bf16[128,256]{1,0:T(8,128)(2,1)}) %reduce-scatter.21.cloned.1.call-update) | async-done | bytes 65552 | tf_op jit(solution)/shard_map/reduce_scatter | solution.py:194
  940.1 159.9 %reduce-scatter.25.cloned.1.call-done = bf16[128,256]{1,0:T(8,128)(2,1)} async-done(((bf16[4096,256]{1,0:T(8,128)(2,1)}), bf16[128,256]{1,0:T(8,128)(2,1)}) %reduce-scatter.25.cloned.1.call-update) | async-done | bytes 65552 | tf_op jit(solution)/shard_map/reduce_scatter | solution.py:194
  1102.0 159.7 %reduce-scatter.23.cloned.1.call-done = bf16[128,256]{1,0:T(8,128)(2,1)} async-done(((bf16[4096,256]{1,0:T(8,128)(2,1)}), bf16[128,256]{1,0:T(8,128)(2,1)}) %reduce-scatter.23.cloned.1.call-update) | async-done | bytes 65552 | tf_op jit(solution)/shard_map/reduce_scatter | solution.py:191
  1262.5 161.4 %reduce-scatter.19.cloned.1.call-done = bf16[128,256]{1,0:T(8,128)(2,1)} async-done(((bf16[4096,256]{1,0:T(8,128)(2,1)}), bf16[128,256]{1,0:T(8,128)(2,1)}) %reduce-scatter.19.cloned.1.call-update) | async-done | bytes 65552 | tf_op jit(solution)/shard_map/reduce_scatter | solution.py:191
  1445.9 35.2 %reduce-scatter.41.cloned.1.call-done = bf16[256,640]{1,0:T(8,128)(2,1)} async-done(((bf16[1024,640]{1,0:T(8,128)(2,1)}), bf16[256,640]{1,0:T(8,128)(2,1)}) %reduce-scatter.41.cloned.1.call-update) | async-done | bytes 327696 | tf_op jit(solution)/shard_map/reduce_scatter | solution.py:325
  1481.1 35.6 %reduce-scatter.39.cloned.1.call-done = bf16[256,640]{1,0:T(8,128)(2,1)} async-done(((bf16[1024,640]{1,0:T(8,128)(2,1)}), bf16[256,640]{1,0:T(8,128)(2,1)}) %reduce-scatter.39.cloned.1.call-update) | async-done | bytes 327696 | tf_op jit(solution)/shard_map/reduce_scatter | solution.py:325
  1516.7 36.0 %reduce-scatter.27.cloned.1.call-done = bf16[640,256]{1,0:T(8,128)(2,1)} async-done(((bf16[640,1024]{1,0:T(8,128)(2,1)}), bf16[640,256]{1,0:T(8,128)(2,1)}) %reduce-scatter.27.cloned.1.call-update) | async-done | bytes 327696 | tf_op jit(solution)/shard_map/reduce_scatter | solution.py:316
  1552.7 36.2 %reduce-scatter.29.cloned.1.call-done = bf16[640,256]{1,0:T(8,128)(2,1)} async-done(((bf16[640,1024]{1,0:T(8,128)(2,1)}), bf16[640,256]{1,0:T(8,128)(2,1)}) %reduce-scatter.29.cloned.1.call-update) | async-done | bytes 327696 | tf_op jit(solution)/shard_map/reduce_scatter | solution.py:316
  1588.8 29.2 %reduce-scatter.35.cloned.1.call-done = bf16[640,64]{0,1:T(8,128)(2,1)} async-done(((bf16[640,256]{0,1:T(8,128)(2,1)}), bf16[640,64]{0,1:T(8,128)(2,1)}) %reduce-scatter.35.cloned.1.call-update) | async-done | bytes 81936 | tf_op jit(solution)/shard_map/reduce_scatter | solution.py:322
  1618.0 30.2 %reduce-scatter.37.cloned.1.call-done = bf16[640,64]{0,1:T(8,128)(2,1)} async-done(((bf16[640,256]{0,1:T(8,128)(2,1)}), bf16[640,64]{0,1:T(8,128)(2,1)}) %reduce-scatter.37.cloned.1.call-update) | async-done | bytes 81936 | tf_op jit(solution)/shard_map/reduce_scatter | solution.py:322
  1648.2 29.8 %reduce-scatter.33.cloned.1.call-done = bf16[640,64]{0,1:T(8,128)(2,1)} async-done(((bf16[640,256]{0,1:T(8,128)(2,1)}), bf16[640,64]{0,1:T(8,128)(2,1)}) %reduce-scatter.33.cloned.1.call-update) | async-done | bytes 81936 | tf_op jit(solution)/shard_map/reduce_scatter | solution.py:319
  1678.0 30.2 %reduce-scatter.31.cloned.1.call-done = bf16[640,64]{0,1:T(8,128)(2,1)} async-done(((bf16[640,256]{0,1:T(8,128)(2,1)}), bf16[640,64]{0,1:T(8,128)(2,1)}) %reduce-scatter.31.cloned.1.call-update) | async-done | bytes 81936 | tf_op jit(solution)/shard_map/reduce_scatter | solution.py:319
  1708.2 43.7 %reduce-scatter.51.cloned.1.call-done = bf16[512,640]{1,0:T(8,128)(2,1)} async-done(((bf16[2048,640]{1,0:T(8,128)(2,1)}), bf16[512,640]{1,0:T(8,128)(2,1)}) %reduce-scatter.51.cloned.1.call-update) | async-done | bytes 655376 | tf_op jit(solution)/shard_map/reduce_scatter | solution.py:334
  1751.9 43.9 %reduce-scatter.53.cloned.1.call-done = bf16[512,640]{1,0:T(8,128)(2,1)} async-done(((bf16[2048,640]{1,0:T(8,128)(2,1)}), bf16[512,640]{1,0:T(8,128)(2,1)}) %reduce-scatter.53.cloned.1.call-update) | async-done | bytes 655376 | tf_op jit(solution)/shard_map/reduce_scatter | solution.py:334
  1795.7 43.5 %reduce-scatter.47.cloned.1.call-done = bf16[640,512]{1,0:T(8,128)(2,1)} async-done(((bf16[640,2048]{1,0:T(8,128)(2,1)}), bf16[640,512]{1,0:T(8,128)(2,1)}) %reduce-scatter.47.cloned.1.call-update) | async-done | bytes 655376 | tf_op jit(solution)/shard_map/reduce_scatter | solution.py:331
  1839.3 43.9 %reduce-scatter.43.cloned.1.call-done = bf16[640,512]{1,0:T(8,128)(2,1)} async-done(((bf16[640,2048]{1,0:T(8,128)(2,1)}), bf16[640,512]{1,0:T(8,128)(2,1)}) %reduce-scatter.43.cloned.1.call-update) | async-done | bytes 655376 | tf_op jit(solution)/shard_map/reduce_scatter | solution.py:328
  1883.1 43.5 %reduce-scatter.49.cloned.1.call-done = bf16[640,512]{1,0:T(8,128)(2,1)} async-done(((bf16[640,2048]{1,0:T(8,128)(2,1)}), bf16[640,512]{1,0:T(8,128)(2,1)}) %reduce-scatter.49.cloned.1.call-update) | async-done | bytes 655376 | tf_op jit(solution)/shard_map/reduce_scatter | solution.py:331
  1926.7 43.7 %reduce-scatter.45.cloned.1.call-done = bf16[640,512]{1,0:T(8,128)(2,1)} async-done(((bf16[640,2048]{1,0:T(8,128)(2,1)}), bf16[640,512]{1,0:T(8,128)(2,1)}) %reduce-scatter.45.cloned.1.call-update) | async-done | bytes 655376 | tf_op jit(solution)/shard_map/reduce_scatter | solution.py:328
  1990.6 69.9 %all-reduce.12 = (bf16[160]{0:T(256)(128)(2,1)S(1)}, bf16[160]{0:T(256)(128)(2,1)S(1)}, bf16[160]{0:T(256)(128)(2,1)S(1)}, bf16[160]{0:T(256)(128)(2,1)S(1)}, bf...) all-reduce(bf16[160]{0:T(256)(128)(2,1)S(1)} %dynamic-slice.7, ...), channel_id=1, replica_groups=mesh['ctx'=32,'fsdp'=4] {'ctx'}, use_global_device_ids=true, to_apply=%region_59.60 | all-reduce | flops 1280 | bytes 5120 | tf_op jit(solution)/shard_map/psum | solution.py:371
  2062.8 224.4 %all-reduce.18.cloned.1.call-done = (bf16[640,256]{1,0:T(8,128)(2,1)}, bf16[640,256]{1,0:T(8,128)(2,1)}, bf16[640,64]{0,1:T(8,128)(2,1)}, bf16[640,64]{0,1:T(8,1...) async-done(((bf16[640,256]{1,0:T(8,128)(2,1)}, ...) | async-done | bytes 5570576 | tf_op jit(solution)/shard_map/psum | solution.py:364
  (383 shorter events, 217.3 us)
Async XLA Ops:
  7.2 55.6 %all-gather.14.cloned.1.call-start = ((), (), s32[]{:S(2)}) async-start(), calls=%async_computation.20 | async-start | bytes 1638400 | tf_op jit(solution)/shard_map/all_gather | solution.py:279
  7.9 165.2 %all-gather.12.cloned.1.call-start = ((), (), s32[]{:S(2)}) async-start(), calls=%async_computation.19 | async-start | bytes 2162688 | tf_op jit(solution)/shard_map/all_gather | solution.py:97
  10.8 783.2 %copy-start.69 = (pred[128]{0:T(512)(128)(4,1)}, pred[128]{0:T(512)(128)(4,1)S(1)}, u32[]{:S(2)}) copy-start(pred[128]{0:T(512)(128)(4,1)S(1)} %get-tuple-element.71) | copy-start | bytes 388
  41.6 287.2 %all-gather.10.cloned.1.call-start = ((), (), s32[]{:S(2)}) async-start(), calls=%async_computation.18 | async-start | bytes 2162688 | tf_op jit(solution)/shard_map/all_gather | solution.py:98
  51.5 322.2 %all-gather.16.cloned.1.call-start = ((), (), s32[]{:S(2)}) async-start(), calls=%async_computation.21 | async-start | bytes 1638400 | tf_op jit(solution)/shard_map/all_gather | solution.py:282
  52.1 455.3 %all-gather.26.cloned.1.call-start = ((), (), s32[]{:S(2)}) async-start(), calls=%async_computation.26 | async-start | bytes 2162688 | tf_op jit(solution)/shard_map/all_gather | solution.py:97
  52.8 610.0 %all-gather.24.cloned.1.call-start = ((), (), s32[]{:S(2)}) async-start(), calls=%async_computation.25 | async-start | bytes 2162688 | tf_op jit(solution)/shard_map/all_gather | solution.py:98
  54.7 660.6 %all-gather.18.cloned.1.call-start = ((), (), s32[]{:S(2)}) async-start(), calls=%async_computation.22 | async-start | bytes 3276800 | tf_op jit(solution)/shard_map/all_gather | solution.py:283
  55.4 690.6 %all-gather.20.cloned.1.call-start = ((), (), s32[]{:S(2)}) async-start(), calls=%async_computation.23 | async-start | bytes 3276800 | tf_op jit(solution)/shard_map/all_gather | solution.py:284
  56.2 720.6 %all-gather.22.cloned.1.call-start = ((), (), s32[]{:S(2)}) async-start(), calls=%async_computation.24 | async-start | bytes 3276800 | tf_op jit(solution)/shard_map/all_gather | solution.py:285
  56.9 881.2 %reduce-scatter.21.cloned.1.call-start = ((), (), s32[]{:S(2)}) async-start(), calls=%async_computation.28 | async-start | bytes 2162688 | tf_op jit(solution)/shard_map/reduce_scatter | solution.py:194
  57.9 736.1 %copy-start.70 = (pred[128]{0:T(512)(128)(4,1)}, pred[128]{0:T(512)(128)(4,1)S(1)}, u32[]{:S(2)}) copy-start(pred[128]{0:T(512)(128)(4,1)S(1)} %broadcast_compare_fusion.2) | copy-start | bytes 388
  799.8 300.2 %reduce-scatter.25.cloned.1.call-start = ((), (), s32[]{:S(2)}) async-start(), calls=%async_computation.30 | async-start | bytes 2162688 | tf_op jit(solution)/shard_map/reduce_scatter | solution.py:194
  808.5 453.1 %reduce-scatter.23.cloned.1.call-start = ((), (), s32[]{:S(2)}) async-start(), calls=%async_computation.29 | async-start | bytes 2162688 | tf_op jit(solution)/shard_map/reduce_scatter | solution.py:191
  833.7 590.1 %reduce-scatter.19.cloned.1.call-start = ((), (), s32[]{:S(2)}) async-start(), calls=%async_computation.27 | async-start | bytes 2162688 | tf_op jit(solution)/shard_map/reduce_scatter | solution.py:191
  859.3 621.8 %reduce-scatter.41.cloned.1.call-start = ((), (), s32[]{:S(2)}) async-start(), calls=%async_computation.38 | async-start | bytes 1638400 | tf_op jit(solution)/shard_map/reduce_scatter | solution.py:325
  861.0 655.7 %reduce-scatter.39.cloned.1.call-start = ((), (), s32[]{:S(2)}) async-start(), calls=%async_computation.37 | async-start | bytes 1638400 | tf_op jit(solution)/shard_map/reduce_scatter | solution.py:325
  862.6 690.1 %reduce-scatter.27.cloned.1.call-start = ((), (), s32[]{:S(2)}) async-start(), calls=%async_computation.31 | async-start | bytes 1638400 | tf_op jit(solution)/shard_map/reduce_scatter | solution.py:316
  904.9 683.9 %reduce-scatter.29.cloned.1.call-start = ((), (), s32[]{:S(2)}) async-start(), calls=%async_computation.32 | async-start | bytes 1638400 | tf_op jit(solution)/shard_map/reduce_scatter | solution.py:316
  911.1 706.9 %reduce-scatter.35.cloned.1.call-start = ((), (), s32[]{:S(2)}) async-start(), calls=%async_computation.35 | async-start | bytes 409600 | tf_op jit(solution)/shard_map/reduce_scatter | solution.py:322
  940.0 708.1 %reduce-scatter.37.cloned.1.call-start = ((), (), s32[]{:S(2)}) async-start(), calls=%async_computation.36 | async-start | bytes 409600 | tf_op jit(solution)/shard_map/reduce_scatter | solution.py:322
  1101.9 576.1 %reduce-scatter.33.cloned.1.call-start = ((), (), s32[]{:S(2)}) async-start(), calls=%async_computation.34 | async-start | bytes 409600 | tf_op jit(solution)/shard_map/reduce_scatter | solution.py:319
  1426.8 281.4 %reduce-scatter.31.cloned.1.call-start = ((), (), s32[]{:S(2)}) async-start(), calls=%async_computation.33 | async-start | bytes 409600 | tf_op jit(solution)/shard_map/reduce_scatter | solution.py:319
  1427.9 324.0 %reduce-scatter.51.cloned.1.call-start = ((), (), s32[]{:S(2)}) async-start(), calls=%async_computation.43 | async-start | bytes 3276800 | tf_op jit(solution)/shard_map/reduce_scatter | solution.py:334
  1431.2 364.5 %reduce-scatter.53.cloned.1.call-start = ((), (), s32[]{:S(2)}) async-start(), calls=%async_computation.44 | async-start | bytes 3276800 | tf_op jit(solution)/shard_map/reduce_scatter | solution.py:334
  1434.6 404.7 %reduce-scatter.47.cloned.1.call-start = ((), (), s32[]{:S(2)}) async-start(), calls=%async_computation.41 | async-start | bytes 3276800 | tf_op jit(solution)/shard_map/reduce_scatter | solution.py:331
  1437.1 446.1 %reduce-scatter.43.cloned.1.call-start = ((), (), s32[]{:S(2)}) async-start(), calls=%async_computation.39 | async-start | bytes 3276800 | tf_op jit(solution)/shard_map/reduce_scatter | solution.py:328
  1439.6 487.1 %reduce-scatter.49.cloned.1.call-start = ((), (), s32[]{:S(2)}) async-start(), calls=%async_computation.42 | async-start | bytes 3276800 | tf_op jit(solution)/shard_map/reduce_scatter | solution.py:331
  1443.3 527.1 %reduce-scatter.45.cloned.1.call-start = ((), (), s32[]{:S(2)}) async-start(), calls=%async_computation.40 | async-start | bytes 3276800 | tf_op jit(solution)/shard_map/reduce_scatter | solution.py:328
  1445.8 614.7 %copy-start.72 = (f32[128]{0:T(128)S(1)}, f32[128]{0:T(128)}, u32[]{:S(2)}) copy-start(f32[128]{0:T(128)} %copy-done.71) | copy-start | bytes 1540
  1445.8 614.7 %copy-start.30 = (f32[128,640]{1,0:T(8,128)S(1)}, f32[128,640]{1,0:T(8,128)}, u32[]{:S(2)}) copy-start(f32[128,640]{1,0:T(8,128)} %copy-done.29) | copy-start | bytes 983044
  1445.9 841.3 %all-reduce.18.cloned.1.call-start = ((), (), s32[]{:S(2)}) async-start(), calls=%async_computation.45 | async-start | bytes 11141120 | tf_op jit(solution)/shard_map/psum | solution.py:364
  (92 other events, 13462.4 us)
Sparse Core Ops, SparseCore 0:
  9.7 27.7 all-gather.13
  41.7 131.4 all-gather.11
  175.4 153.3 all-gather.9
  330.3 43.4 all-gather.15
  375.8 131.4 all-gather.25
  509.4 153.3 all-gather.23
  664.4 50.8 all-gather.17
  717.0 29.0 all-gather.19
  747.7 29.0 all-gather.21
  799.9 138.1 reduce-scatter.20
  940.6 159.3 reduce-scatter.24
  1102.2 159.3 reduce-scatter.22
  1264.1 159.6 reduce-scatter.18
  1426.9 54.1 reduce-scatter.40
  1483.8 32.8 reduce-scatter.38
  1519.8 32.8 reduce-scatter.26
  1555.9 32.8 reduce-scatter.28
  1591.3 26.6 reduce-scatter.34
  1621.4 26.7 reduce-scatter.36
  1651.2 26.7 reduce-scatter.32
  1681.3 26.7 reduce-scatter.30
  1710.8 41.0 reduce-scatter.50
  1754.7 40.9 reduce-scatter.52
  1798.2 40.9 reduce-scatter.46
  1842.1 40.9 reduce-scatter.42
  1885.6 40.9 reduce-scatter.48
  1929.4 40.9 reduce-scatter.44
  1974.2 312.9 all-reduce.17
where the time goes:
time: 2330 us; the launch traced here: 2310 us
  waiting for transfers between devices  1930 us (83%)
  matrix products  188 us (8%)
  blocking collectives  112 us (5%)
  other arithmetic  42.1 us (2%)
    reduce_scatter x2, waiting for transfers between devices, micro_step(): lax.psum_scatter(key_terms.astype(jnp.bfloat16), 'ctx', scatter_dimension...  321 us
    all_gather x2, waiting for transfers between devices, micro_step(): lax.all_gather(value_rows, 'ctx', axis=0, tiled=True)  295 us
    all_gather x2, waiting for transfers between devices, micro_step(): lax.all_gather(key_rows, 'ctx', axis=0, tiled=True)  239 us
    psum x1, waiting for transfers between devices, on_device(): lax.psum(piece_q.astype(jnp.bfloat16), 'ctx').astype(jnp.float32)  224 us
    reduce_scatter x2, waiting for transfers between devices, micro_step(): lax.psum_scatter(value_terms.astype(jnp.bfloat16), 'ctx', scatter_dimensi...  187 us
    reduce_scatter x2, waiting for transfers between devices, on_device(): lax.psum_scatter(term_d.astype(jnp.bfloat16), 'fsdp', scatter_dimension=0...  87.6 us
    reduce_scatter x2, waiting for transfers between devices, on_device(): lax.psum_scatter(term_g.astype(jnp.bfloat16), 'fsdp', scatter_dimension=1...  87.6 us
    reduce_scatter x2, waiting for transfers between devices, on_device(): lax.psum_scatter(term_u.astype(jnp.bfloat16), 'fsdp', scatter_dimension=1...  87.1 us
  transfers between devices with their start and end apart: 28, of which 27 were waited for; matrix products, arithmetic and copies ran while one was open for 9% of the time, Pallas kernels for 0%

commit v1 on v0

v1 whole, which is shorter than its diff:
```python
import functools

import jax
import jax.numpy as jnp
import numpy as np
from jax import lax
from jax.experimental import pallas as pl
from jax.experimental.pallas import tpu as pltpu
from jax.sharding import PartitionSpec as P

F32, BF16 = jnp.float32, jnp.bfloat16
CAP = 50.0
EPS = 1e-06
BASE = 1000000.0
HD = 256
HALF = HD // 2
BLK = 64
CHUNK = 512
AXES = ("ctx", "fsdp")
VMEM_LIMIT = 50 * 1024 * 1024


def all_places():
    for yl in range(2):
        for z in range(4):
            for x in range(4):
                for yh in range(2):
                    for c in range(2):
                        yield yl, z, x, yh, c


def flat(yl, z, x, yh, c):
    return (((yl * 4 + z) * 4 + x) * 2 + yh) * 2 + c


def send(array, move):
    pairs = [(flat(*p), flat(*move(*p))) for p in all_places()]
    return lax.ppermute(array, AXES, pairs)


def to_core(yl, z, x, yh, c):
    return yl, z, x, yh, 1 - c


def to_next(yl, z, x, yh, c):
    return 1 - yl, z, x, 1 - yh, c


def to_yl(yl, z, x, yh, c):
    return 1 - yl, z, x, yh, c


def to_yh(yl, z, x, yh, c):
    return yl, z, x, 1 - yh, c


def regroup(turn):
    def move(yl, z, x, yh, c):
        zh, zl, xh, xl = z // 2, z % 2, x // 2, x % 2
        return yl, c * 2 + zl, (xh ^ turn) * 2 + xl, yh, zh

    return move


def to_cube(step):
    dy, dz, dx = step >> 2, (step >> 1) & 1, step & 1

    def move(yl, z, x, yh, c):
        return yl ^ dy, z ^ dz, x ^ dx, yh, c

    return move


PLANE = [[yl * 16 + i for i in range(16)] for yl in range(2)]


def swap_plane(array):
    return lax.all_to_all(
        array, "ctx", split_axis=0, concat_axis=0, axis_index_groups=PLANE, tiled=True
    )


def inverse_rms(values):
    return lax.rsqrt(jnp.mean(values * values, axis=-1, keepdims=True) + EPS)


def norm_back(values, gain, grads):
    scale = inverse_rms(values)
    hat = values * scale
    scaled = grads * (1.0 + gain)
    inner = jnp.mean(scaled * hat, axis=-1, keepdims=True)
    return scale * (scaled - hat * inner), jnp.sum(grads * hat, axis=0)


def dot(left, right):
    return jnp.dot(left, right, preferred_element_type=F32)


def dot_nt(left, right):
    return lax.dot_general(left, right, (((1,), (1,)), ((), ())), preferred_element_type=F32)


def dot_tn(left, right):
    return lax.dot_general(left, right, (((0,), (0,)), ((), ())), preferred_element_type=F32)


def angle_tables():
    freqs = BASE ** (-(np.arange(HALF, dtype=np.float32) * 2.0 / HD)).astype(np.float32)
    coarse = (np.arange(64, dtype=np.float64) * 64)[:, None] * freqs[None, :].astype(np.float64)
    fine = np.arange(BLK, dtype=np.float64)[:, None] * freqs[None, :].astype(np.float64)
    tables = [np.cos(coarse), np.sin(coarse), np.cos(fine), np.sin(fine)]
    return np.stack(tables).astype(np.float32)


def chunk_tables(tables, chunk):
    rows = pl.ds(pl.multiple_of(chunk * 8, 8), 8)
    ca = tables[0, rows, :][:, None, :]
    sa = tables[1, rows, :][:, None, :]
    cb = tables[2][None]
    sb = tables[3][None]
    cosine = (ca * cb - sa * sb).reshape(CHUNK, HALF)
    sine = (sa * cb + ca * sb).reshape(CHUNK, HALF)
    return cosine, sine


def tile_facts(meta, t):
    b0, b1 = meta[72 + 2 * t], meta[73 + 2 * t]
    p0, p1 = meta[80 + 2 * t], meta[81 + 2 * t]
    length = meta[64]
    last = jnp.minimum(p1 * BLK + BLK, length)
    chunks = jnp.where(p0 * BLK < length, (last + CHUNK - 1) // CHUNK, 0)
    lane = lax.broadcasted_iota(jnp.int32, (1, 4 * BLK), 1)
    second = (lane // BLK) % 2 == 1
    limit = jnp.where(second, p1, p0) * BLK + lane % BLK
    return b0, b1, chunks, jnp.minimum(limit, length - 1)


def chunks_needed(meta):
    most = jnp.int32(0)
    for t in range(4):
        most = jnp.maximum(most, tile_facts(meta, t)[2])
    return most


def rows_of(chunk):
    return pl.ds(pl.multiple_of(chunk * CHUNK, CHUNK), CHUNK)


def tile_rows(ref, b0, b1):
    return jnp.concatenate([ref[0, b0], ref[0, b1], ref[1, b0], ref[1, b1]], axis=0)


def put_tile(ref, b0, b1, tile):
    ref[0, b0] = tile[0:BLK]
    ref[0, b1] = tile[BLK : 2 * BLK]
    ref[1, b0] = tile[2 * BLK : 3 * BLK]
    ref[1, b1] = tile[3 * BLK :]


def load_sorted(meta, pieces, sorted_ref, sem):
    for n, piece in enumerate(pieces):
        for b in range(4):
            at = pl.multiple_of(meta[n * 4 + b] * BLK, BLK)
            pltpu.make_async_copy(
                piece.at[pl.ds(b * BLK, BLK), :], sorted_ref.at[pl.ds(at, BLK), :], sem
            ).start()


def attend_kernel(meta, q_ref, w_ref, tables, *refs):
    pieces = refs[:16]
    o_ref, ot_ref, inv_ref, k_out, v_out = refs[16:21]
    normed, keys, values, values_t, acc, total, in_sem, k_sem, v_sem = refs[21:]
    load_sorted(meta, pieces, normed, in_sem)
    pltpu.make_async_copy(normed, normed, in_sem).wait()

    def prepare(chunk, carry):
        rows = rows_of(chunk)
        both = dot(normed[rows, :], w_ref[...])
        cosine, sine = chunk_tables(tables, chunk)
        first, second = both[:, :HALF], both[:, HALF:HD]
        keys[rows, :HALF] = (first * cosine - second * sine).astype(BF16)
        keys[rows, HALF:] = (second * cosine + first * sine).astype(BF16)
        low = both[:, HD:].astype(BF16)
        values[rows, :] = low
        values_t[chunk] = low.T
        return carry

    lax.fori_loop(0, chunks_needed(meta), prepare, 0)
    k_copy = pltpu.make_async_copy(keys, k_out, k_sem)
    v_copy = pltpu.make_async_copy(values, v_out, v_sem)
    k_copy.start()
    v_copy.start()

    def tile(t, carry):
        b0, b1, chunks, limit = tile_facts(meta, t)
        queries = tile_rows(q_ref, b0, b1)
        acc[...] = jnp.zeros_like(acc)
        total[...] = jnp.zeros_like(total)

        def step(chunk, inner):
            scores = dot_nt(keys[rows_of(chunk), :], queries)
            grown = jnp.exp(CAP * jnp.tanh(scores * (1.0 / CAP)))
            at = chunk * CHUNK + lax.broadcasted_iota(jnp.int32, (CHUNK, 4 * BLK), 0)
            grown = jnp.where(at <= limit, grown, 0.0)
            total[...] += jnp.sum(grown.reshape(CHUNK // 8, 8, 4 * BLK), axis=0)
            acc[...] += dot(values_t[chunk], grown.astype(BF16))
            return inner

        lax.fori_loop(0, chunks, step, 0)
        whole = jnp.sum(total[...], axis=0, keepdims=True)
        inverse = jnp.where(whole > 0.0, 1.0 / jnp.where(whole > 0.0, whole, 1.0), 0.0)
        mixed = acc[...] * inverse
        inv_ref[t] = jnp.broadcast_to(inverse, (8, 4 * BLK))
        ot_ref[t] = mixed.astype(BF16)
        put_tile(o_ref, b0, b1, mixed.T.astype(BF16))
        return carry

    lax.fori_loop(0, 4, tile, 0)
    k_copy.wait()
    v_copy.wait()


def attend_back_kernel(meta, q_ref, do_ref, ot_ref, inv_ref, k_ref, v_ref, tables, *refs):
    pieces = refs[:16]
    dq_ref, grad_ref, own_ref, oth_ref = refs[16:20]
    normed, keys_t, d_keys, d_values, d_both, acc, in_sem, out_sem = refs[20:]
    load_sorted(meta, pieces, normed, in_sem)
    needed = chunks_needed(meta)

    def prepare(chunk, carry):
        rows = rows_of(chunk)
        keys_t[chunk] = k_ref[rows, :].T
        d_keys[rows, :] = jnp.zeros((CHUNK, HD), F32)
        d_values[rows, :] = jnp.zeros((CHUNK, HD), F32)
        return carry

    lax.fori_loop(0, needed, prepare, 0)

    def tile(t, carry):
        b0, b1, chunks, limit = tile_facts(meta, t)
        queries = tile_rows(q_ref, b0, b1)
        grads = tile_rows(do_ref, b0, b1)
        inverse = inv_ref[t, 0:1, :]
        grads_t = grads.astype(F32).T
        center = jnp.sum(grads_t * ot_ref[t].astype(F32), axis=0, keepdims=True)
        acc[...] = jnp.zeros_like(acc)

        def step(chunk, inner):
            rows = rows_of(chunk)
            scores = dot_nt(k_ref[rows, :], queries)
            ratio = jnp.tanh(scores * (1.0 / CAP))
            probs = jnp.exp(CAP * ratio) * inverse
            at = chunk * CHUNK + lax.broadcasted_iota(jnp.int32, (CHUNK, 4 * BLK), 0)
            probs = jnp.where(at <= limit, probs, 0.0)
            d_probs = dot_nt(v_ref[rows, :], grads)
            d_scores = (probs * (d_probs - center) * (1.0 - ratio * ratio)).astype(BF16)
            d_values[rows, :] += dot(probs.astype(BF16), grads)
            d_keys[rows, :] += dot(d_scores, queries)
            acc[...] += dot(keys_t[chunk], d_scores)
            return inner

        lax.fori_loop(0, chunks, step, 0)
        put_tile(dq_ref, b0, b1, acc[...].T)
        return carry

    lax.fori_loop(0, 4, tile, 0)
    pltpu.make_async_copy(normed, normed, in_sem).wait()
    grad_ref[...] = jnp.zeros_like(grad_ref)

    def finish(chunk, carry):
        rows = rows_of(chunk)
        cosine, sine = chunk_tables(tables, chunk)
        first, second = d_keys[rows, :HALF], d_keys[rows, HALF:]
        d_both[rows, :HALF] = (first * cosine + second * sine).astype(BF16)
        d_both[rows, HALF:HD] = (second * cosine - first * sine).astype(BF16)
        d_both[rows, HD:] = d_values[rows, :].astype(BF16)
        grad_ref[...] += dot_tn(normed[rows, :], d_both[rows, :])
        return carry

    lax.fori_loop(0, needed, finish, 0)

    def clear(chunk, carry):
        d_both[rows_of(chunk), :] = jnp.zeros((CHUNK, 2 * HD), BF16)
        return carry

    lax.fori_loop(needed, 8, clear, 0)
    for n in range(16):
        target = own_ref if n < 8 else oth_ref
        for b in range(4):
            at = pl.multiple_of(meta[n * 4 + b] * BLK, BLK)
            pltpu.make_async_copy(
                d_both.at[pl.ds(at, BLK), :], target.at[n % 8, pl.ds(b * BLK, BLK), :], out_sem
            ).start()
    pltpu.make_async_copy(d_both, d_both, out_sem).wait()


SMEM_SPEC = pl.BlockSpec(memory_space=pltpu.SMEM)
VMEM_SPEC = pl.BlockSpec(memory_space=pltpu.VMEM)
ANY_SPEC = pl.BlockSpec(memory_space=pl.ANY)
SLOTS = 4096


def attend(meta, queries, key_value_weight, tables, pieces):
    width = pieces[0].shape[1]
    return pl.pallas_call(
        attend_kernel,
        out_shape=(
            jax.ShapeDtypeStruct((2, 8, BLK, HD), BF16),
            jax.ShapeDtypeStruct((4, HD, 4 * BLK), BF16),
            jax.ShapeDtypeStruct((4, 8, 4 * BLK), F32),
            jax.ShapeDtypeStruct((SLOTS, HD), BF16),
            jax.ShapeDtypeStruct((SLOTS, HD), BF16),
        ),
        in_specs=[SMEM_SPEC, VMEM_SPEC, VMEM_SPEC, VMEM_SPEC] + [ANY_SPEC] * 16,
        out_specs=(VMEM_SPEC, VMEM_SPEC, VMEM_SPEC, ANY_SPEC, ANY_SPEC),
        scratch_shapes=[
            pltpu.VMEM((SLOTS, width), BF16),
            pltpu.VMEM((SLOTS, HD), BF16),
            pltpu.VMEM((SLOTS, HD), BF16),
            pltpu.VMEM((SLOTS // CHUNK, HD, CHUNK), BF16),
            pltpu.VMEM((HD, 4 * BLK), F32),
            pltpu.VMEM((8, 4 * BLK), F32),
            pltpu.SemaphoreType.DMA,
            pltpu.SemaphoreType.DMA,
            pltpu.SemaphoreType.DMA,
        ],
        compiler_params=pltpu.CompilerParams(vmem_limit_bytes=VMEM_LIMIT),
        cost_estimate=pl.CostEstimate(
            flops=8 * 10**9, bytes_accessed=16 * 10**6, transcendentals=8 * 10**6
        ),
        name="attend",
    )(meta, queries, key_value_weight, tables, *pieces)


def attend_back(meta, queries, d_attended, mixed_t, inverse, keys, values, tables, pieces):
    width = pieces[0].shape[1]
    return pl.pallas_call(
        attend_back_kernel,
        out_shape=(
            jax.ShapeDtypeStruct((2, 8, BLK, HD), F32),
            jax.ShapeDtypeStruct((width, 2 * HD), F32),
            jax.ShapeDtypeStruct((8, 4 * BLK, 2 * HD), BF16),
            jax.ShapeDtypeStruct((8, 4 * BLK, 2 * HD), BF16),
        ),
        in_specs=[SMEM_SPEC] + [VMEM_SPEC] * 7 + [ANY_SPEC] * 16,
        out_specs=(VMEM_SPEC, VMEM_SPEC, ANY_SPEC, ANY_SPEC),
        scratch_shapes=[
            pltpu.VMEM((SLOTS, width), BF16),
            pltpu.VMEM((SLOTS // CHUNK, HD, CHUNK), BF16),
            pltpu.VMEM((SLOTS, HD), F32),
            pltpu.VMEM((SLOTS, HD), F32),
            pltpu.VMEM((SLOTS, 2 * HD), BF16),
            pltpu.VMEM((HD, 4 * BLK), F32),
            pltpu.SemaphoreType.DMA,
            pltpu.SemaphoreType.DMA,
        ],
        compiler_params=pltpu.CompilerParams(vmem_limit_bytes=VMEM_LIMIT),
        cost_estimate=pl.CostEstimate(
            flops=20 * 10**9, bytes_accessed=24 * 10**6, transcendentals=8 * 10**6
        ),
        name="attend_back",
    )(meta, queries, d_attended, mixed_t, inverse, keys, values, tables, *pieces)


def sum_shards(own, other):
    rows, cols = own.shape
    both = jnp.concatenate([own, other], axis=1).astype(BF16)
    got = swap_plane(both.reshape(16, rows // 16, 2 * cols))
    part = jnp.sum(got.astype(F32), axis=0).astype(BF16)
    mine, theirs = part[:, :cols], part[:, cols:]
    total = (
        mine.astype(F32)
        + send(mine, to_yl).astype(F32)
        + send(theirs, to_next).astype(F32)
        + send(theirs, to_yh).astype(F32)
    ).astype(BF16)
    everyone = swap_plane(jnp.broadcast_to(total[None], (16, rows // 16, cols)))
    return everyone.reshape(rows, cols)


def on_device(
    tokens,
    cotangent,
    lengths,
    block_order,
    query_weight,
    key_weight,
    value_weight,
    out_weight,
    gate_weight,
    up_weight,
    down_weight,
    gain_attn_in,
    gain_attn_out,
    gain_ffn_in,
    gain_ffn_out,
):
    ctx, fsdp = lax.axis_index("ctx"), lax.axis_index("fsdp")
    yl, z, x = ctx // 16, (ctx // 4) % 4, ctx % 4
    yh, c = fsdp // 2, fsdp % 2
    zh, zl, xh, xl = z // 2, z % 2, x // 2, x % 2
    low_y, low_c, low_x = yh == 0, c == 0, xh == 0
    own_rows = 4 * BLK
    width = tokens.shape[-1]

    def gather_rows(array):
        pieces = (
            send(jnp.where(low_x, array[0, 0], array[0, 1]), regroup(0)),
            send(jnp.where(low_x, array[0, 1], array[0, 0]), regroup(1)),
        )
        return jnp.concatenate(pieces, axis=0)

    def return_rows(rows):
        first = send(rows[: own_rows // 2], regroup(0))
        second = send(rows[own_rows // 2 :], regroup(1))
        return jnp.stack([jnp.where(low_x, first, second), jnp.where(low_x, second, first)])[None]

    rows_in = gather_rows(tokens)

    gains = jnp.stack([gain_attn_in, gain_attn_out, gain_ffn_in, gain_ffn_out])
    gains_next = send(gains, to_next)
    half_gains = jnp.stack(
        [jnp.where(low_y, gains, gains_next), jnp.where(low_y, gains_next, gains)]
    )
    half_other = send(half_gains, to_core)
    quarters = jnp.stack(
        [jnp.where(low_c, half_gains, half_other), jnp.where(low_c, half_other, half_gains)], axis=1
    )
    all_gains = jnp.transpose(quarters, (2, 0, 1, 3)).reshape(4, width).astype(F32)
    gain_a, gain_b, gain_c, gain_d = (all_gains[i] for i in range(4))

    lengths_other = send(lengths, to_core)
    lengths_here = jnp.where(zh == c, lengths, lengths_other)
    length = jnp.where(low_x, lengths_here[0, 0], lengths_here[0, 1])

    qkv_own = jnp.concatenate([query_weight, key_weight, value_weight], axis=1)
    qkv_next = send(qkv_own, to_next)
    heads = HD
    kv_low = jnp.where(low_y, qkv_own[:, heads:], qkv_next[:, heads:])
    kv_high = jnp.where(low_y, qkv_next[:, heads:], qkv_own[:, heads:])
    kv_pair = jnp.stack([kv_low, kv_high])
    kv_pair_other = send(kv_pair, to_core)
    kv_c0 = jnp.where(low_c, kv_pair, kv_pair_other)
    kv_c1 = jnp.where(low_c, kv_pair_other, kv_pair)
    quarter = key_weight.shape[1]
    kv_weight = jnp.concatenate(
        [m[:, :quarter] for m in (kv_c0[0], kv_c1[0], kv_c0[1], kv_c1[1])]
        + [m[:, quarter:] for m in (kv_c0[0], kv_c1[0], kv_c0[1], kv_c1[1])],
        axis=1,
    )
    q_own, q_next = qkv_own[:, :heads], qkv_next[:, :heads]

    do_own = jnp.concatenate([down_weight, out_weight], axis=0)
    do_next = send(do_own, to_next)
    gu_own = jnp.concatenate([gate_weight, up_weight], axis=1)
    gu_next = send(gu_own, to_next)
    hidden_cols = gate_weight.shape[1]
    down_own, out_own = do_own[:hidden_cols], do_own[hidden_cols:]
    down_next, out_next = do_next[:hidden_cols], do_next[hidden_cols:]

    stored = []
    for other in range(2):
        for step in range(8):
            dy, dz, dx = step >> 2, (step >> 1) & 1, step & 1
            for turn in range(2):
                place = (yl ^ dy) * 16 + ((c ^ other) * 2 + (zl ^ dz)) * 4
                place = place + (xh ^ turn) * 2 + (xl ^ dx)
                stored += [place * 2, place * 2 + 1]
    stored = jnp.stack(stored)
    slots = jnp.arange(64, dtype=jnp.int32)
    block_at = jnp.sum(
        jnp.where(stored[:, None] == slots[None, :], block_order[None, :], 0), axis=1
    ).astype(jnp.int32)
    q_blocks = jnp.concatenate([block_at[0:4], block_at[32:36]])
    rank = jnp.sum((q_blocks[None, :] < q_blocks[:, None]).astype(jnp.int32), axis=1)
    eight = jnp.arange(8, dtype=jnp.int32)
    chosen = rank[None, :] == eight[:, None]
    order = jnp.sum(jnp.where(chosen, eight[None, :], 0), axis=1).astype(jnp.int32)
    order_block = jnp.sum(jnp.where(chosen, q_blocks[None, :], 0), axis=1).astype(jnp.int32)
    meta = jnp.concatenate(
        [block_at, jnp.full((8,), length, jnp.int32), order, order_block]
    )
    row_pos = (q_blocks[:, None] * BLK + jnp.arange(BLK, dtype=jnp.int32)[None, :]).reshape(-1)
    valid = (row_pos[:own_rows] < length)[:, None]

    start = rows_in.astype(F32)
    normed_own = (start * inverse_rms(start) * (1.0 + gain_a)).astype(BF16)
    near = [normed_own] + [send(normed_own, to_cube(step)) for step in range(1, 8)]
    far = [send(piece, to_core) for piece in near]
    pieces = near + far
    normed = jnp.concatenate([near[0], far[0]], axis=0)

    freqs = BASE ** (-(jnp.arange(HALF).astype(F32) * 2.0 / HD))
    angles = row_pos.astype(F32)[:, None] * freqs[None, :]
    cosine, sine = jnp.cos(angles), jnp.sin(angles)

    def rotated(pre):
        first, second = pre[:, :HALF], pre[:, HALF:]
        turned = jnp.concatenate(
            [first * cosine - second * sine, second * cosine + first * sine], axis=1
        )
        return (turned * HD ** (-0.5)).astype(BF16)

    queries = jnp.stack([rotated(dot(normed, q_own)), rotated(dot(normed, q_next))])
    queries = queries.reshape(2, 8, BLK, HD)
    tables = jnp.asarray(angle_tables())
    mixed, mixed_t, inverse, keys, values = attend(meta, queries, kv_weight, tables, pieces)
    mixed = mixed.reshape(2, 2 * own_rows, HD)

    def share(partial):
        return partial[:own_rows] + send(partial[own_rows:].astype(BF16), to_core).astype(F32)

    def both_cores(rows):
        return jnp.concatenate([rows, send(rows, to_core)], axis=0)

    branch = share(dot(mixed[0], out_own) + dot(mixed[1], out_next))
    middle = start + branch * inverse_rms(branch) * (1.0 + gain_b)
    second = both_cores((middle * inverse_rms(middle) * (1.0 + gain_c)).astype(BF16))

    def gelu_product(gate_up):
        return jax.nn.gelu(gate_up[:, :hidden_cols], approximate=True) * gate_up[:, hidden_cols:]

    gate_up_own, gate_up_next = dot(second, gu_own), dot(second, gu_next)
    hidden_own, pull_own = jax.vjp(gelu_product, gate_up_own)
    hidden_next, pull_next = jax.vjp(gelu_product, gate_up_next)
    hidden_own, hidden_next = hidden_own.astype(BF16), hidden_next.astype(BF16)
    output = share(dot(hidden_own, down_own) + dot(hidden_next, down_next))
    result = jnp.where(valid, middle + output * inverse_rms(output) * (1.0 + gain_d), 0.0)
    result_block = return_rows(result.astype(BF16))

    seed = jnp.where(valid, gather_rows(cotangent).astype(F32), 0.0)
    d_output, d_gain_d = norm_back(output, gain_d, seed)
    d_output = both_cores(d_output.astype(BF16))
    d_gu_own = pull_own(dot_nt(d_output, down_own))[0].astype(BF16)
    d_gu_next = pull_next(dot_nt(d_output, down_next))[0].astype(BF16)
    d_second = share(dot_nt(d_gu_own, gu_own) + dot_nt(d_gu_next, gu_next))
    d_mid, d_gain_c = norm_back(middle, gain_c, d_second)
    d_middle = seed + d_mid
    d_branch, d_gain_b = norm_back(branch, gain_b, d_middle)
    d_branch = both_cores(d_branch.astype(BF16))
    d_mixed = jnp.stack([dot_nt(d_branch, out_own), dot_nt(d_branch, out_next)]).astype(BF16)

    grads_own = jnp.concatenate(
        [dot_tn(second, d_gu_own), dot_tn(d_output, hidden_own), dot_tn(d_branch, mixed[0])], axis=1
    )
    grads_next = jnp.concatenate(
        [dot_tn(second, d_gu_next), dot_tn(d_output, hidden_next), dot_tn(d_branch, mixed[1])], axis=1
    )
    ffn_sum = sum_shards(grads_own, grads_next)

    d_queries, kv_grad, d_near, d_far = attend_back(
        meta,
        queries,
        d_mixed.reshape(2, 8, BLK, HD),
        mixed_t,
        inverse,
        keys,
        values,
        tables,
        pieces,
    )
    chip_sum = (d_near.astype(F32) + send(d_far, to_core).astype(F32)).astype(BF16)
    d_kv = chip_sum[0].astype(F32)
    for step in range(1, 8):
        d_kv = d_kv + send(chip_sum[step], to_cube(step)).astype(F32)
    d_kv = d_kv.astype(BF16)

    def unrotated(turned):
        scaled = turned.reshape(2 * own_rows, HD) * HD ** (-0.5)
        first, second = scaled[:, :HALF], scaled[:, HALF:]
        return jnp.concatenate(
            [first * cosine + second * sine, second * cosine - first * sine], axis=1
        ).astype(BF16)

    d_q_own, d_q_next = unrotated(d_queries[0]), unrotated(d_queries[1])
    d_normed = share(dot_nt(d_q_own, q_own) + dot_nt(d_q_next, q_next))
    d_normed = d_normed + dot_nt(d_kv, kv_weight)
    d_start, _ = norm_back(start, gain_a, d_normed)
    token_block = return_rows((d_middle + d_start).astype(BF16)).astype(F32)

    q_grad_own, q_grad_next = dot_tn(normed, d_q_own), dot_tn(normed, d_q_next)
    split = kv_grad.reshape(width, 2, 2, 2, quarter)
    keep = jnp.where(low_c, split[:, :, :, 0], split[:, :, :, 1])
    give = jnp.where(low_c, split[:, :, :, 1], split[:, :, :, 0])
    keep = keep + send(give.astype(BF16), to_core).astype(F32)
    kv_grad_own = jnp.where(low_y, keep[:, :, 0], keep[:, :, 1]).reshape(width, 2 * quarter)
    kv_grad_next = jnp.where(low_y, keep[:, :, 1], keep[:, :, 0]).reshape(width, 2 * quarter)
    qkv_grad_own = jnp.concatenate([q_grad_own, kv_grad_own], axis=1)
    qkv_grad_next = jnp.concatenate([q_grad_next, kv_grad_next], axis=1)
    d_gain_a = jnp.sum(qkv_own.astype(F32) * qkv_grad_own, axis=1)
    d_gain_a = d_gain_a + jnp.sum(qkv_next.astype(F32) * qkv_grad_next, axis=1)
    d_gain_a = d_gain_a / (1.0 + gain_a)
    d_gains = jnp.stack([d_gain_a, d_gain_b, d_gain_c, d_gain_d])
    d_gains = (d_gains + send(d_gains.astype(BF16), to_core).astype(F32)).T
    qkv_sum = sum_shards(
        jnp.concatenate([qkv_grad_own, d_gains], axis=1),
        jnp.concatenate([qkv_grad_next, d_gains], axis=1),
    ).astype(F32)
    share_rows = width // 4
    gain_grads = lax.dynamic_slice_in_dim(qkv_sum[:, -4:], fsdp * share_rows, share_rows, axis=0)
    ffn_sum = ffn_sum.astype(F32)
    at_v = heads + quarter
    return (
        result_block,
        token_block,
        qkv_sum[:, :heads],
        qkv_sum[:, heads:at_v],
        qkv_sum[:, at_v : at_v + quarter],
        ffn_sum[:, 3 * hidden_cols :].T,
        ffn_sum[:, :hidden_cols],
        ffn_sum[:, hidden_cols : 2 * hidden_cols],
        ffn_sum[:, 2 * hidden_cols : 3 * hidden_cols].T,
        gain_grads[:, 0],
        gain_grads[:, 1],
        gain_grads[:, 2],
        gain_grads[:, 3],
    )


def solution(mesh):
    rows, cols, first = P("fsdp", None, "ctx", None), P(None, "fsdp"), P("fsdp", None)
    weights = (cols, cols, cols, first, cols, cols, first)
    gains = (P("fsdp"),) * 4
    return jax.shard_map(
        on_device,
        mesh=mesh,
        in_specs=(rows, rows, first, P()) + weights + gains,
        out_specs=(rows, rows) + weights + gains,
        check_vma=False,
    )
```

time: 2330 us -> 456 us (0.20)
  waiting for transfers between devices: 1930 us -> 151 us
  matrix products: 188 us -> 36.8 us
  blocking collectives: 112 us -> 0 us
  starting transfers between devices: 2.24 us -> 109 us
  Pallas kernels: 0 us -> 58.3 us
  local copies, waits for them, and re-layouts: 15.9 us -> 50.3 us
    reduce_scatter x18 -> x0, waiting for transfers between devices: 1030 us -> none  [the longest x2 321 us: micro_step(): lax.psum_scatter(key_terms.astype(jnp.bfloat16), 'ctx', scatter_dimension...]
    all_gather x9 -> x0, waiting for transfers between devices: 668 us -> none  [the longest x2 295 us: micro_step(): lax.all_gather(value_rows, 'ctx', axis=0, tiled=True)]
    psum x1 -> x0, waiting for transfers between devices: 224 us -> none  [on_device(): lax.psum(piece_q.astype(jnp.bfloat16), 'ctx').astype(jnp.float32)]
    dot_general x54 -> x25, matrix products: 188 us -> 36.8 us  [the longest x9 15.5 us: dot_nt(): lax.dot_general(left, right, (((1,), (1,)), ((), ())), preferred_element_...]
    ppermute x0 -> x53, waiting for transfers between devices: none -> 105 us  [send(): return lax.ppermute(array, AXES, pairs)]
    ppermute x0 -> x53, starting transfers between devices: none -> 87.7 us  [send(): return lax.ppermute(array, AXES, pairs)]
    psum x1 -> x0, blocking collectives: 69.9 us -> none  [on_device(): lax.psum(piece_ga.astype(jnp.bfloat16), 'ctx').astype(jnp.float32)]
    pallas_call x0 -> x2, Pallas kernels: none -> 58.3 us  [the longest x1 33 us: attend_back(): pl.pallas_call(attend_back_kernel, out_shape=(jax.ShapeDtypeStruct((2, 8,...]
  transfers between devices with their start and end apart: 28 -> 57, of which waited for: 27 -> 17; matrix products, arithmetic and copies ran while one was open for 9% -> 16% of each run, Pallas kernels for 0% -> 6%
where the time goes in v1:
time: 456 us; the launch traced here: 447 us
  waiting for transfers between devices  151 us (33%)
  starting transfers between devices  109 us (24%)
  Pallas kernels  58.3 us (13%)
  local copies, waits for them, and re-layouts  50.3 us (11%)
  other arithmetic  37.5 us (8%)
  matrix products  36.8 us (8%)
    ppermute x53, waiting for transfers between devices, send(): return lax.ppermute(array, AXES, pairs)  105 us
    ppermute x53, starting transfers between devices, send(): return lax.ppermute(array, AXES, pairs)  87.7 us
    all_to_all x4, waiting for transfers between devices, swap_plane(): lax.all_to_all(array, 'ctx', split_axis=0, concat_axis=0, axis_index_grou...  46.4 us
    pallas_call x1, Pallas kernels, attend_back(): pl.pallas_call(attend_back_kernel, out_shape=(jax.ShapeDtypeStruct((2, 8,...  33 us
    pallas_call x1, Pallas kernels, attend(): pl.pallas_call(attend_kernel, out_shape=(jax.ShapeDtypeStruct((2, 8, BLK,...  25.2 us
    all_to_all x4, starting transfers between devices, swap_plane(): lax.all_to_all(array, 'ctx', split_axis=0, concat_axis=0, axis_index_grou...  21 us
    unnamed x179, local copies, waits for them, and re-layouts  20.5 us
    dot_general x9, matrix products, dot_nt(): lax.dot_general(left, right, (((1,), (1,)), ((), ())), preferred_element_...  15.5 us
  transfers between devices with their start and end apart: 57, of which 17 were waited for; matrix products, arithmetic and copies ran while one was open for 16% of the time, Pallas kernels for 6%

profile of v1, /device:TPU:1, one launch (start us, length us, event | category | flops | bytes accessed | tf_op | source)
XLA Modules:
  0.0 446.6 jit_solution(14290803159542291786)
XLA Ops:
  4.8 2.9 collective-permute-start.3
  8.8 5.7 %collective-permute-start.1 = (bf16[128,640]{1,0:T(8,128)(2,1)S(1)}, bf16[128,640]{1,0:T(8,128)(2,1)S(1)}, u32[]{:S(2)}, u32[]{:S(2)}) collective-permute-start(bf16[128,640]{1,0:T(8,128)(2,1)S(1)} %get-tuple-element.180), channel_id=1, source_target_pairs={{0,0},{1,32},{2,2},{3,34},{4,4},{5,36},{6,6},{7,38},{8,8},{9,40},{... | collective-permute-start | bytes 491528 | tf_op jit(solution)/shard_map/ppermute | solution.py:38
  38.5 18.2 %collective-permute-done.13.refs_6_ = bf16[256,640]{1,0:T(8,128)(2,1)S(1)} collective-permute-done((bf16[256,640]{1,0:T(8,128)(2,1)S(1)}, bf16[256,640]{1,0:T(8,128)(2,1)S(1)}, u32[]{:S(2)}, u32[]{:S(2)}) %collective-permute-start.13) | collective-permute-done | bytes 327712 | tf_op jit(solution)/shard_map/ppermute | solution.py:38
  58.5 3.0 collective-permute-done.11.refs_4_
  73.4 25.2 %attend.1 = (bf16[2,8,64,256]{3,2,1,0:T(8,128)(2,1)}, bf16[4,256,256]{2,1,0:T(8,128)(2,1)}, f32[4,8,256]{2,1,0:T(8,128)S(1)}, bf16[4096,256]{1,0:T(8,128)(2,1)}, bf16[4096,256]{1,0:T(8,128)(2,1)}) custom-call(s32[88]{0:T(128)S(1)} %pad_add_fusion.1.meta, bf16[2,8,64,256]{3,2,1,0:T(8,128)(2,1)} %pad_maximum_fusion.5.q_ref, ...), custom_call_target="tpu_custom_call" | custom-call | flops 8000000000 | bytes 16000000 | tf_op jit(solution)/shard_map/attend/pallas_call | solution.py:305
  108.8 27.0 %collective-permute-done.25 = bf16[640,1024]{1,0:T(8,128)(2,1)} collective-permute-done((bf16[640,1024]{1,0:T(8,128)(2,1)}, bf16[640,1024]{1,0:T(8,128)(2,1)}, u32[]{:S(2)}, u32[]{:S(2)}) %collective-permute-start.25) | collective-permute-done | bytes 1310752 | tf_op jit(solution)/shard_map/ppermute | solution.py:38
  149.1 2.8 collective-permute-start.29
  151.9 3.9 collective-permute-start.30
  157.9 3.7 collective-permute-done.30
  167.6 3.1 fusion.57
  175.6 3.1 convolution_add_fusion.1
  193.6 33.0 %attend_back.1 = (f32[2,8,64,256]{3,2,1,0:T(8,128)}, f32[640,512]{1,0:T(8,128)}, bf16[8,256,512]{2,1,0:T(8,128)(2,1)}, bf16[8,256,512]{2,1,0:T(8,128)(2,1)}) custom-call(s32[88]{0:T(128)S(1)} %pad_add_fusion.1.meta, bf16[2,8,64,256]{3,2,1,0:T(8,128)(2,1)} %pad_maximum_fusion.5.q_ref, bf16[2,8,64,256]{3,2,1,0:T(8,128)(2,1)} %pad_maximum_fusion.6.do_ref, ...), custom_call_target="tpu_custom_call" | custom-call | flops 20000000000 | bytes 24000000 | tf_op jit(solution)/shard_map/attend_back/pallas_call | solution.py:337
  241.5 2.6 concatenate.148
  244.2 4.7 %all-to-all-start = ((bf16[16,40,776]{2,1,0:T(8,128)(2,1)}), bf16[16,40,776]{2,1,0:T(8,128)(2,1)S(1)}, u32[]{:S(2)}, u32[]{:S(2)}) async-start(bf16[16,40,776]{2,1,0:T(8,128)(2,1)} %concatenate.148), calls=%async_computation | async-start | bytes 2293760 | tf_op jit(solution)/shard_map/all_to_all | solution.py:78
  253.3 2.6 constant_dynamic-update-slice_fusion.3
  258.4 8.0 %all-to-all-done = bf16[16,40,776]{2,1,0:T(8,128)(2,1)S(1)} async-done(((bf16[16,40,776]{2,1,0:T(8,128)(2,1)}), bf16[16,40,776]{2,1,0:T(8,128)(2,1)S(1)}, u32[]{:S(2)}, u32[]{:S(2)}) %all-to-all-start) | async-done | bytes 993312 | tf_op jit(solution)/shard_map/all_to_all | solution.py:78
  266.4 4.8 %all-to-all-start.2 = ((bf16[16,40,3584]{2,1,0:T(8,128)(2,1)}), bf16[16,40,3584]{2,1,0:T(8,128)(2,1)}, u32[]{:S(2)}, u32[]{:S(2)}) async-start(bf16[16,40,3584]{2,1,0:T(8,128)(2,1)} %fusion), calls=%async_computation.2 | async-start | bytes 9175040 | tf_op jit(solution)/shard_map/all_to_all | solution.py:78
  274.1 4.9 %collective-permute-start.27 = (bf16[128,640]{1,0:T(8,128)(2,1)}, bf16[128,640]{1,0:T(8,128)(2,1)}, u32[]{:S(2)}, u32[]{:S(2)}) collective-permute-start(bf16[128,640]{1,0:T(8,128)(2,1)} %get-tuple-element.174), channel_id=1, source_target_pairs={{0,0},{1,32},{2,2},{3,34},{4,4},{5,36},{6,6},{7,38},{8,8},{9,40},{... | collective-permute-start | bytes 491528 | tf_op jit(solution)/shard_map/ppermute | solution.py:38
  281.9 6.6 %collective-permute-start.48 = (bf16[40,388]{1,0:T(8,128)(2,1)S(1)}, bf16[40,388]{1,0:T(8,128)(2,1)S(1)}, u32[]{:S(2)}, u32[]{:S(2)}) collective-permute-start(bf16[40,388]{1,0:T(8,128)(2,1)S(1)} %get-tuple-element.193), channel_id=1, source_target_pairs={{0,66},{1,67},{2,64},{3,65},{4,70},{5,71},{6,68},{7,69},{8,74},{9,... | collective-permute-start | bytes 93128 | tf_op jit(solution)/shard_map/ppermute | solution.py:38
  291.8 4.2 collective-permute-start.28
  298.2 38.3 %all-to-all-done.2 = bf16[16,40,3584]{2,1,0:T(8,128)(2,1)} async-done(((bf16[16,40,3584]{2,1,0:T(8,128)(2,1)}), bf16[16,40,3584]{2,1,0:T(8,128)(2,1)}, u32[]{:S(2)}, u32[]{:S(2)}) %all-to-all-start.2) | async-done | bytes 4587552 | tf_op jit(solution)/shard_map/all_to_all | solution.py:78
  337.4 5.2 %all-to-all-start.1 = ((bf16[16,40,388]{2,1,0:T(8,128)(2,1)}), bf16[16,40,388]{2,1,0:T(8,128)(2,1)S(1)}, u32[]{:S(2)}, u32[]{:S(2)}) async-start(bf16[16,40,388]{2,1,0:T(8,128)(2,1)} %broadcast_in_dim.60), calls=%async_computation.1 | async-start | bytes 1310720 | tf_op jit(solution)/shard_map/all_to_all | solution.py:78
  342.7 3.0 reduce_sum.211
  347.0 6.5 %collective-permute-start.51 = (bf16[40,1792]{1,0:T(8,128)(2,1)S(1)}, bf16[40,1792]{1,0:T(8,128)(2,1)S(1)}, u32[]{:S(2)}, u32[]{:S(2)}) collective-permute-start(bf16[40,1792]{1,0:T(8,128)(2,1)S(1)} %get-tuple-element.183), channel_id=1, source_target_pairs={{0,66},{1,67},{2,64},{3,65},{4,70},{5,71},{6,68},{7,69},{8,74},{9,... | collective-permute-start | bytes 430088 | tf_op jit(solution)/shard_map/ppermute | solution.py:38
  355.1 2.9 collective-permute-done.50
  358.0 5.2 %collective-permute-start.34 = (bf16[256,640]{1,0:T(8,128)(2,1)}, bf16[256,640]{1,0:T(8,128)(2,1)}, u32[]{:S(2)}, u32[]{:S(2)}) collective-permute-start(bf16[256,640]{1,0:T(8,128)(2,1)} %slice.577), channel_id=1, source_target_pairs={{0,1},{1,0},{2,3},{3,2},{4,5},{5,4},{6,7},{7,6},{8,9},{9,8},{10,11... | collective-permute-start | bytes 983048 | tf_op jit(solution)/shard_map/ppermute | solution.py:38
  367.5 6.2 %all-to-all-start.3 = ((bf16[16,40,1792]{2,1,0:T(8,128)(2,1)}), bf16[16,40,1792]{2,1,0:T(8,128)(2,1)S(1)}, u32[]{:S(2)}, u32[]{:S(2)}) async-start(bf16[16,40,1792]{2,1,0:T(8,128)(2,1)} %broadcast_in_dim.61), calls=%async_computation.3 | async-start | bytes 4587520 | tf_op jit(solution)/shard_map/all_to_all | solution.py:78
  383.0 5.1 %collective-permute-done.41 = bf16[256,512]{1,0:T(8,128)(2,1)S(1)} collective-permute-done((bf16[256,512]{1,0:T(8,128)(2,1)S(1)}, bf16[256,512]{1,0:T(8,128)(2,1)S(1)}, u32[]{:S(2)}, u32[]{:S(2)}) %collective-permute-start.41) | collective-permute-done | bytes 262176 | tf_op jit(solution)/shard_map/ppermute | solution.py:38
  388.1 26.5 %collective-permute-done.40 = bf16[256,512]{1,0:T(8,128)(2,1)S(1)} collective-permute-done((bf16[256,512]{1,0:T(8,128)(2,1)S(1)}, bf16[256,512]{1,0:T(8,128)(2,1)S(1)}, u32[]{:S(2)}, u32[]{:S(2)}) %collective-permute-start.40) | collective-permute-done | bytes 262176 | tf_op jit(solution)/shard_map/ppermute | solution.py:38
  414.6 8.3 %collective-permute-done.38 = bf16[256,512]{1,0:T(8,128)(2,1)S(1)} collective-permute-done((bf16[256,512]{1,0:T(8,128)(2,1)S(1)}, bf16[256,512]{1,0:T(8,128)(2,1)S(1)}, u32[]{:S(2)}, u32[]{:S(2)}) %collective-permute-start.38) | collective-permute-done | bytes 262176 | tf_op jit(solution)/shard_map/ppermute | solution.py:38
  425.7 4.7 %collective-permute-start.43 = (bf16[128,640]{1,0:T(8,128)(2,1)}, bf16[128,640]{1,0:T(8,128)(2,1)}, u32[]{:S(2)}, u32[]{:S(2)}) collective-permute-start(bf16[128,640]{1,0:T(8,128)(2,1)} %get-tuple-element.168), channel_id=1, source_target_pairs={{0,0},{1,32},{2,2},{3,34},{4,4},{5,36},{6,6},{7,38},{8,8},{9,40},{... | collective-permute-start | bytes 491528 | tf_op jit(solution)/shard_map/ppermute | solution.py:38
  435.3 3.9 collective-permute-done.44
  (414 shorter events, 156.8 us)
Async XLA Ops:
  0.7 21.7 %collective-permute-start = (s32[1,2]{1,0:T(1,128)}, s32[1,2]{1,0:T(1,128)S(1)}, u32[]{:S(2)}, u32[]{:S(2)}) collective-permute-start(s32[1,2]{1,0:T(1,128)} %param.18), channel_id=1, source_target_pairs={{0,1},{1,0},{2,3},{3,2},{4,5},{5,4},{6,7},{7,6},{8,9},{9,8},{10,11... | collective-permute-start | bytes 32 | tf_op jit(solution)/shard_map/ppermute | solution.py:38
  4.8 19.5 %collective-permute-start.3 = (bf16[4,160]{1,0:T(4,128)(2,1)S(1)}, bf16[4,160]{1,0:T(4,128)(2,1)S(1)}, u32[]{:S(2)}, u32[]{:S(2)}) collective-permute-start(bf16[4,160]{1,0:T(4,128)(2,1)S(1)} %pad_maximum_fusion.22), channel_id=1, source_target_pairs={{0,66},{1,67},{2,64},{3,65},{4,70},{5,71},{6,68},{7,69},{8,74},{9,... | collective-permute-start | bytes 3848 | tf_op jit(solution)/shard_map/ppermute | solution.py:38
  8.8 16.9 %collective-permute-start.1 = (bf16[128,640]{1,0:T(8,128)(2,1)S(1)}, bf16[128,640]{1,0:T(8,128)(2,1)S(1)}, u32[]{:S(2)}, u32[]{:S(2)}) collective-permute-start(bf16[128,640]{1,0:T(8,128)(2,1)S(1)} %get-tuple-element.180), channel_id=1, source_target_pairs={{0,0},{1,32},{2,2},{3,34},{4,4},{5,36},{6,6},{7,38},{8,8},{9,40},{... | collective-permute-start | bytes 491528 | tf_op jit(solution)/shard_map/ppermute | solution.py:38
  14.5 11.2 %collective-permute-start.2 = (bf16[128,640]{1,0:T(8,128)(2,1)S(1)}, bf16[128,640]{1,0:T(8,128)(2,1)S(1)}, u32[]{:S(2)}, u32[]{:S(2)}) collective-permute-start(bf16[128,640]{1,0:T(8,128)(2,1)S(1)} %get-tuple-element.181), channel_id=1, source_target_pairs={{0,8},{1,40},{2,10},{3,42},{4,12},{5,44},{6,14},{7,46},{8,0},{9,32... | collective-permute-start | bytes 491528 | tf_op jit(solution)/shard_map/ppermute | solution.py:38
  26.1 12.0 %collective-permute-start.14 = (bf16[256,640]{1,0:T(8,128)(2,1)S(1)}, bf16[256,640]{1,0:T(8,128)(2,1)S(1)}, u32[]{:S(2)}, u32[]{:S(2)}) collective-permute-start(bf16[256,640]{1,0:T(8,128)(2,1)S(1)} %fusion.19.refs_0_), channel_id=1, source_target_pairs={{0,84},{1,85},{2,86},{3,87},{4,80},{5,81},{6,82},{7,83},{8,92},{9,... | collective-permute-start | bytes 983048 | tf_op jit(solution)/shard_map/ppermute | solution.py:38
  26.9 29.9 %collective-permute-start.13 = (bf16[256,640]{1,0:T(8,128)(2,1)S(1)}, bf16[256,640]{1,0:T(8,128)(2,1)S(1)}, u32[]{:S(2)}, u32[]{:S(2)}) collective-permute-start(bf16[256,640]{1,0:T(8,128)(2,1)S(1)} %fusion.19.refs_0_), channel_id=1, source_target_pairs={{0,80},{1,81},{2,82},{3,83},{4,84},{5,85},{6,86},{7,87},{8,88},{9,... | collective-permute-start | bytes 983048 | tf_op jit(solution)/shard_map/ppermute | solution.py:38
  28.5 29.1 %collective-permute-start.12 = (bf16[256,640]{1,0:T(8,128)(2,1)S(1)}, bf16[256,640]{1,0:T(8,128)(2,1)S(1)}, u32[]{:S(2)}, u32[]{:S(2)}) collective-permute-start(bf16[256,640]{1,0:T(8,128)(2,1)S(1)} %fusion.19.refs_0_), channel_id=1, source_target_pairs={{0,68},{1,69},{2,70},{3,71},{4,64},{5,65},{6,66},{7,67},{8,76},{9,... | collective-permute-start | bytes 983048 | tf_op jit(solution)/shard_map/ppermute | solution.py:38
  29.3 32.1 %collective-permute-start.11 = (bf16[256,640]{1,0:T(8,128)(2,1)S(1)}, bf16[256,640]{1,0:T(8,128)(2,1)S(1)}, u32[]{:S(2)}, u32[]{:S(2)}) collective-permute-start(bf16[256,640]{1,0:T(8,128)(2,1)S(1)} %fusion.19.refs_0_), channel_id=1, source_target_pairs={{0,64},{1,65},{2,66},{3,67},{4,68},{5,69},{6,70},{7,71},{8,72},{9,... | collective-permute-start | bytes 983048 | tf_op jit(solution)/shard_map/ppermute | solution.py:38
  36.9 27.3 %collective-permute-start.10 = (bf16[256,640]{1,0:T(8,128)(2,1)S(1)}, bf16[256,640]{1,0:T(8,128)(2,1)S(1)}, u32[]{:S(2)}, u32[]{:S(2)}) collective-permute-start(bf16[256,640]{1,0:T(8,128)(2,1)S(1)} %fusion.19.refs_0_), channel_id=1, source_target_pairs={{0,20},{1,21},{2,22},{3,23},{4,16},{5,17},{6,18},{7,19},{8,28},{9,... | collective-permute-start | bytes 983048 | tf_op jit(solution)/shard_map/ppermute | solution.py:38
  38.1 26.1 %collective-permute-start.9 = (bf16[256,640]{1,0:T(8,128)(2,1)S(1)}, bf16[256,640]{1,0:T(8,128)(2,1)S(1)}, u32[]{:S(2)}, u32[]{:S(2)}) collective-permute-start(bf16[256,640]{1,0:T(8,128)(2,1)S(1)} %fusion.19.refs_0_), channel_id=1, source_target_pairs={{0,16},{1,17},{2,18},{3,19},{4,20},{5,21},{6,22},{7,23},{8,24},{9,... | collective-permute-start | bytes 983048 | tf_op jit(solution)/shard_map/ppermute | solution.py:38
  71.4 28.5 %collective-permute-start.22 = (bf16[768,640]{1,0:T(8,128)(2,1)}, bf16[768,640]{1,0:T(8,128)(2,1)S(1)}, u32[]{:S(2)}, u32[]{:S(2)}) collective-permute-start(bf16[768,640]{1,0:T(8,128)(2,1)} %pad_maximum_fusion), channel_id=1, source_target_pairs={{0,66},{1,67},{2,64},{3,65},{4,70},{5,71},{6,68},{7,69},{8,74},{9,... | collective-permute-start | bytes 2949128 | tf_op jit(solution)/shard_map/ppermute | solution.py:38
  104.0 31.8 %collective-permute-start.25 = (bf16[640,1024]{1,0:T(8,128)(2,1)}, bf16[640,1024]{1,0:T(8,128)(2,1)}, u32[]{:S(2)}, u32[]{:S(2)}) collective-permute-start(bf16[640,1024]{1,0:T(8,128)(2,1)} %constant_dynamic-update-slice_fusion), channel_id=1, source_target_pairs={{0,66},{1,67},{2,64},{3,65},{4,70},{5,71},{6,68},{7,69},{8,74},{9,... | collective-permute-start | bytes 3932168 | tf_op jit(solution)/shard_map/ppermute | solution.py:38
  108.2 27.5 %collective-permute-start.24 = (bf16[256,640]{1,0:T(8,128)(2,1)S(1)}, bf16[256,640]{1,0:T(8,128)(2,1)S(1)}, u32[]{:S(2)}, u32[]{:S(2)}) collective-permute-start(bf16[256,640]{1,0:T(8,128)(2,1)S(1)} %multiply_convert_fusion.4), channel_id=1, source_target_pairs={{0,1},{1,0},{2,3},{3,2},{4,5},{5,4},{6,7},{7,6},{8,9},{9,8},{10,11... | collective-permute-start | bytes 983048 | tf_op jit(solution)/shard_map/ppermute | solution.py:38
  244.2 22.2 %all-to-all-start = ((bf16[16,40,776]{2,1,0:T(8,128)(2,1)}), bf16[16,40,776]{2,1,0:T(8,128)(2,1)S(1)}, u32[]{:S(2)}, u32[]{:S(2)}) async-start(bf16[16,40,776]{2,1,0:T(8,128)(2,1)} %concatenate.148), calls=%async_computation | async-start | bytes 2293760 | tf_op jit(solution)/shard_map/all_to_all | solution.py:78
  266.4 70.1 %all-to-all-start.2 = ((bf16[16,40,3584]{2,1,0:T(8,128)(2,1)}), bf16[16,40,3584]{2,1,0:T(8,128)(2,1)}, u32[]{:S(2)}, u32[]{:S(2)}) async-start(bf16[16,40,3584]{2,1,0:T(8,128)(2,1)} %fusion), calls=%async_computation.2 | async-start | bytes 9175040 | tf_op jit(solution)/shard_map/all_to_all | solution.py:78
  271.3 24.7 %collective-permute-start.35 = (bf16[8,256,512]{2,1,0:T(8,128)(2,1)}, bf16[8,256,512]{2,1,0:T(8,128)(2,1)}, u32[]{:S(2)}, u32[]{:S(2)}) collective-permute-start(bf16[8,256,512]{2,1,0:T(8,128)(2,1)} %get-tuple-element.29), channel_id=1, source_target_pairs={{0,1},{1,0},{2,3},{3,2},{4,5},{5,4},{6,7},{7,6},{8,9},{9,8},{10,11... | collective-permute-start | bytes 6291464 | tf_op jit(solution)/shard_map/ppermute | solution.py:38
  274.1 99.6 %collective-permute-start.27 = (bf16[128,640]{1,0:T(8,128)(2,1)}, bf16[128,640]{1,0:T(8,128)(2,1)}, u32[]{:S(2)}, u32[]{:S(2)}) collective-permute-start(bf16[128,640]{1,0:T(8,128)(2,1)} %get-tuple-element.174), channel_id=1, source_target_pairs={{0,0},{1,32},{2,2},{3,34},{4,4},{5,36},{6,6},{7,38},{8,8},{9,40},{... | collective-permute-start | bytes 491528 | tf_op jit(solution)/shard_map/ppermute | solution.py:38
  280.7 15.3 %collective-permute-start.49 = (bf16[40,388]{1,0:T(8,128)(2,1)S(1)}, bf16[40,388]{1,0:T(8,128)(2,1)S(1)}, u32[]{:S(2)}, u32[]{:S(2)}) collective-permute-start(bf16[40,388]{1,0:T(8,128)(2,1)S(1)} %get-tuple-element.193), channel_id=1, source_target_pairs={{0,2},{1,3},{2,0},{3,1},{4,6},{5,7},{6,4},{7,5},{8,10},{9,11},{10,... | collective-permute-start | bytes 93128 | tf_op jit(solution)/shard_map/ppermute | solution.py:38
  281.9 14.1 %collective-permute-start.48 = (bf16[40,388]{1,0:T(8,128)(2,1)S(1)}, bf16[40,388]{1,0:T(8,128)(2,1)S(1)}, u32[]{:S(2)}, u32[]{:S(2)}) collective-permute-start(bf16[40,388]{1,0:T(8,128)(2,1)S(1)} %get-tuple-element.193), channel_id=1, source_target_pairs={{0,66},{1,67},{2,64},{3,65},{4,70},{5,71},{6,68},{7,69},{8,74},{9,... | collective-permute-start | bytes 93128 | tf_op jit(solution)/shard_map/ppermute | solution.py:38
  291.8 82.0 %collective-permute-start.28 = (bf16[128,640]{1,0:T(8,128)(2,1)}, bf16[128,640]{1,0:T(8,128)(2,1)}, u32[]{:S(2)}, u32[]{:S(2)}) collective-permute-start(bf16[128,640]{1,0:T(8,128)(2,1)} %get-tuple-element.175), channel_id=1, source_target_pairs={{0,8},{1,40},{2,10},{3,42},{4,12},{5,44},{6,14},{7,46},{8,0},{9,32... | collective-permute-start | bytes 491528 | tf_op jit(solution)/shard_map/ppermute | solution.py:38
  337.4 28.6 %all-to-all-start.1 = ((bf16[16,40,388]{2,1,0:T(8,128)(2,1)}), bf16[16,40,388]{2,1,0:T(8,128)(2,1)S(1)}, u32[]{:S(2)}, u32[]{:S(2)}) async-start(bf16[16,40,388]{2,1,0:T(8,128)(2,1)} %broadcast_in_dim.60), calls=%async_computation.1 | async-start | bytes 1310720 | tf_op jit(solution)/shard_map/all_to_all | solution.py:78
  345.7 17.4 %collective-permute-start.52 = (bf16[40,1792]{1,0:T(8,128)(2,1)S(1)}, bf16[40,1792]{1,0:T(8,128)(2,1)S(1)}, u32[]{:S(2)}, u32[]{:S(2)}) collective-permute-start(bf16[40,1792]{1,0:T(8,128)(2,1)S(1)} %get-tuple-element.183), channel_id=1, source_target_pairs={{0,2},{1,3},{2,0},{3,1},{4,6},{5,7},{6,4},{7,5},{8,10},{9,11},{10,... | collective-permute-start | bytes 430088 | tf_op jit(solution)/shard_map/ppermute | solution.py:38
  347.0 17.8 %collective-permute-start.51 = (bf16[40,1792]{1,0:T(8,128)(2,1)S(1)}, bf16[40,1792]{1,0:T(8,128)(2,1)S(1)}, u32[]{:S(2)}, u32[]{:S(2)}) collective-permute-start(bf16[40,1792]{1,0:T(8,128)(2,1)S(1)} %get-tuple-element.183), channel_id=1, source_target_pairs={{0,66},{1,67},{2,64},{3,65},{4,70},{5,71},{6,68},{7,69},{8,74},{9,... | collective-permute-start | bytes 430088 | tf_op jit(solution)/shard_map/ppermute | solution.py:38
  358.0 21.2 %collective-permute-start.34 = (bf16[256,640]{1,0:T(8,128)(2,1)}, bf16[256,640]{1,0:T(8,128)(2,1)}, u32[]{:S(2)}, u32[]{:S(2)}) collective-permute-start(bf16[256,640]{1,0:T(8,128)(2,1)} %slice.577), channel_id=1, source_target_pairs={{0,1},{1,0},{2,3},{3,2},{4,5},{5,4},{6,7},{7,6},{8,9},{9,8},{10,11... | collective-permute-start | bytes 983048 | tf_op jit(solution)/shard_map/ppermute | solution.py:38
  363.1 17.2 %collective-permute-start.36 = (bf16[256,512]{1,0:T(8,128)(2,1)}, bf16[256,512]{1,0:T(8,128)(2,1)}, u32[]{:S(2)}, u32[]{:S(2)}) collective-permute-start(bf16[256,512]{1,0:T(8,128)(2,1)} %get-tuple-element.137), channel_id=1, source_target_pairs={{0,4},{1,5},{2,6},{3,7},{4,0},{5,1},{6,2},{7,3},{8,12},{9,13},{10,... | collective-permute-start | bytes 786440 | tf_op jit(solution)/shard_map/ppermute | solution.py:38
  364.8 15.7 %collective-permute-start.42 = (bf16[256,512]{1,0:T(8,128)(2,1)}, bf16[256,512]{1,0:T(8,128)(2,1)}, u32[]{:S(2)}, u32[]{:S(2)}) collective-permute-start(bf16[256,512]{1,0:T(8,128)(2,1)} %get-tuple-element.138), channel_id=1, source_target_pairs={{0,84},{1,85},{2,86},{3,87},{4,80},{5,81},{6,82},{7,83},{8,92},{9,... | collective-permute-start | bytes 786440 | tf_op jit(solution)/shard_map/ppermute | solution.py:38
  367.5 73.5 %all-to-all-start.3 = ((bf16[16,40,1792]{2,1,0:T(8,128)(2,1)}), bf16[16,40,1792]{2,1,0:T(8,128)(2,1)S(1)}, u32[]{:S(2)}, u32[]{:S(2)}) async-start(bf16[16,40,1792]{2,1,0:T(8,128)(2,1)} %broadcast_in_dim.61), calls=%async_computation.3 | async-start | bytes 4587520 | tf_op jit(solution)/shard_map/all_to_all | solution.py:78
  375.7 12.4 %collective-permute-start.41 = (bf16[256,512]{1,0:T(8,128)(2,1)S(1)}, bf16[256,512]{1,0:T(8,128)(2,1)S(1)}, u32[]{:S(2)}, u32[]{:S(2)}) collective-permute-start(bf16[256,512]{1,0:T(8,128)(2,1)S(1)} %copy-done.79), channel_id=1, source_target_pairs={{0,80},{1,81},{2,82},{3,83},{4,84},{5,85},{6,86},{7,87},{8,88},{9,... | collective-permute-start | bytes 786440 | tf_op jit(solution)/shard_map/ppermute | solution.py:38
  378.0 36.6 %collective-permute-start.40 = (bf16[256,512]{1,0:T(8,128)(2,1)S(1)}, bf16[256,512]{1,0:T(8,128)(2,1)S(1)}, u32[]{:S(2)}, u32[]{:S(2)}) collective-permute-start(bf16[256,512]{1,0:T(8,128)(2,1)S(1)} %copy-done.78), channel_id=1, source_target_pairs={{0,68},{1,69},{2,70},{3,71},{4,64},{5,65},{6,66},{7,67},{8,76},{9,... | collective-permute-start | bytes 786440 | tf_op jit(solution)/shard_map/ppermute | solution.py:38
  379.1 35.4 %collective-permute-start.39 = (bf16[256,512]{1,0:T(8,128)(2,1)S(1)}, bf16[256,512]{1,0:T(8,128)(2,1)S(1)}, u32[]{:S(2)}, u32[]{:S(2)}) collective-permute-start(bf16[256,512]{1,0:T(8,128)(2,1)S(1)} %copy-done.77), channel_id=1, source_target_pairs={{0,64},{1,65},{2,66},{3,67},{4,68},{5,69},{6,70},{7,71},{8,72},{9,... | collective-permute-start | bytes 786440 | tf_op jit(solution)/shard_map/ppermute | solution.py:38
  380.4 42.4 %collective-permute-start.38 = (bf16[256,512]{1,0:T(8,128)(2,1)S(1)}, bf16[256,512]{1,0:T(8,128)(2,1)S(1)}, u32[]{:S(2)}, u32[]{:S(2)}) collective-permute-start(bf16[256,512]{1,0:T(8,128)(2,1)S(1)} %copy-done.76), channel_id=1, source_target_pairs={{0,20},{1,21},{2,22},{3,23},{4,16},{5,17},{6,18},{7,19},{8,28},{9,... | collective-permute-start | bytes 786440 | tf_op jit(solution)/shard_map/ppermute | solution.py:38
  380.5 42.3 %collective-permute-start.37 = (bf16[256,512]{1,0:T(8,128)(2,1)S(1)}, bf16[256,512]{1,0:T(8,128)(2,1)S(1)}, u32[]{:S(2)}, u32[]{:S(2)}) collective-permute-start(bf16[256,512]{1,0:T(8,128)(2,1)S(1)} %get-tuple-element.143), channel_id=1, source_target_pairs={{0,16},{1,17},{2,18},{3,19},{4,20},{5,21},{6,22},{7,23},{8,24},{9,... | collective-permute-start | bytes 786440 | tf_op jit(solution)/shard_map/ppermute | solution.py:38
  (109 other events, 763.9 us)
